TPU v7x, 256 devices: a whole 4x4x8 slice. The times are simulated.
256 devices in a mesh: loop: 4 (over y_lo, core), grp: 64 (over y_hi, z, x).
Axes of the slice: x: 4, y: 4 (y_hi: 2, y_lo: 2; y = y_hi * 2 + y_lo), z: 8, core: 2. Of those that a mesh axis runs over, the one named last changes fastest.
Arguments:
- queries: bfloat16 [1, 12, 16, 32, 128], P(None, None, 'loop'), may hold values from -18 to 18
- cache_keys: bfloat16 [1, 12, 131072, 128], P(None, None, ('loop', 'grp')), may hold values from -7 to 7
- cache_values: bfloat16 [1, 12, 131072, 128], P(None, None, ('loop', 'grp')), may hold values from -6 to 6
- draft_keys: bfloat16 [1, 12, 32, 128], replicated, may hold values from -18 to 18
- draft_values: bfloat16 [1, 12, 32, 128], replicated, may hold values from -6 to 6
- tree_mask: int32 [12, 32, 32], replicated, may hold values from 0 to 1, as said below
- valid_length: int32 [12], replicated, may hold values from 65536 to 131072
Outputs:
- attended: bfloat16 [1, 12, 16, 32, 128], P(None, None, 'loop')
Inputs may be any that keep to these rules, and one draw needn't show every extreme that they name: `tree_mask`: row r of each sequence's mask holds 1 at column r and at the columns of every ancestor of draft token r in a tree whose parents precede their children, 0 elsewhere.
All inputs are finite; a program needn't handle non-finite values.
Results may differ from a plain program's by a relative error of at most 0.004.
Values may be sent and summed in bfloat16 or wider, within the bound.
A program may use at most 256 MiB of HBM per device.

v0:
```python
import math

import jax
import jax.numpy as jnp
from jax import lax
from jax.sharding import PartitionSpec as P

FLOOR = -1e30


def from_behind(shard, axis, by):
    count = lax.axis_size(axis)
    return lax.ppermute(shard, axis, [(i, (i + by) % count) for i in range(count)])


def combine_parts(left_part, right_part):
    left_peak, left_total, left_sum = left_part
    right_peak, right_total, right_sum = right_part
    joined = jnp.maximum(left_peak, right_peak)
    left_factor = jnp.exp(left_peak - joined)
    right_factor = jnp.exp(right_peak - joined)
    return (
        joined,
        left_total * left_factor + right_total * right_factor,
        left_sum * left_factor[..., None] + right_sum * right_factor[..., None],
    )


def cache_part(query_rows, cache_keys, cache_values, offset, limits):
    scale = 1.0 / math.sqrt(query_rows.shape[-1])
    positions = offset + lax.iota(jnp.int32, cache_keys.shape[2])
    usable = positions[None, :] < limits[:, None]

    def one_sequence(items):
        query_block, key_block, value_block, usable_row = items
        scores = (
            lax.dot_general(
                query_block, key_block, (((1,), (1,)), ((), ())), preferred_element_type=jnp.float32
            )
            * scale
        )
        peak = jnp.max(jnp.where(usable_row[None, :], scores, FLOOR), axis=1)
        weights = jnp.where(usable_row[None, :], jnp.exp(scores - peak[:, None]), 0.0).astype(
            jnp.bfloat16
        )
        total = jnp.sum(weights, axis=1, dtype=jnp.float32)
        summed = jnp.dot(weights, value_block, preferred_element_type=jnp.float32)
        return (peak, total, summed)

    peak, total, summed = lax.map(
        one_sequence, (query_rows[0], cache_keys[0], cache_values[0], usable)
    )
    peaks = [peak]
    totals = [total]
    sums = [summed]
    return (jnp.stack(peaks, 0), jnp.stack(totals, 0), jnp.stack(sums, 0))


def draft_part(query_rows, draft_keys, draft_values, tree_mask, heads, active):
    scale = 1.0 / math.sqrt(query_rows.shape[-1])
    allowed = ((jnp.tile(tree_mask, (1, heads, 1)) == 1) & active)[None, :, :, :]
    scores = (
        jnp.einsum("lsqd,lsrd->lsqr", query_rows, draft_keys, preferred_element_type=jnp.float32)
        * scale
    )
    peak = jnp.max(jnp.where(allowed, scores, FLOOR), axis=3)
    weights = jnp.where(allowed, jnp.exp(scores - peak[..., None]), 0.0).astype(jnp.bfloat16)
    total = jnp.sum(weights, axis=3, dtype=jnp.float32)
    summed = jnp.einsum(
        "lsqr,lsrd->lsqd", weights, draft_values, preferred_element_type=jnp.float32
    )
    return (peak, total, summed)


def group_reduce(partial_value):
    peak = lax.pmax(partial_value[0], "grp")
    factor = jnp.exp(partial_value[0] - peak)
    total, summed = lax.psum(
        (partial_value[1] * factor, partial_value[2] * factor[..., None]), "grp"
    )
    return (peak, total, summed)


def local(queries, cache_keys, cache_values, draft_keys, draft_values, tree_mask, valid_length):
    layers, seqs, local_heads, rows, width = queries.shape
    loop_size = lax.axis_size("loop")
    group_size = lax.axis_size("grp")
    loop_index = lax.axis_index("loop")
    group_index = lax.axis_index("grp")
    offset = (loop_index * group_size + group_index) * cache_keys.shape[2]
    span = local_heads * rows
    travel = queries.reshape(layers, seqs, span, width)
    partial_value = draft_part(
        travel, draft_keys, draft_values, tree_mask, local_heads, group_index == 0
    )
    for turn_index in range(loop_size):
        partial_value = combine_parts(
            partial_value, cache_part(travel, cache_keys, cache_values, offset, valid_length)
        )
        partial_value = from_behind(
            (partial_value[0], partial_value[1], partial_value[2]), "loop", 1
        )
        if turn_index + 1 < loop_size:
            travel = from_behind(travel, "loop", 1)
    peak, total, summed = group_reduce(partial_value)
    attended = (summed / total[..., None]).astype(jnp.bfloat16)
    return attended.reshape(layers, seqs, local_heads, rows, width)


def solution(mesh):
    in_specs = (
        P(None, None, "loop", None, None),
        P(None, None, ("loop", "grp"), None),
        P(None, None, ("loop", "grp"), None),
        P(),
        P(),
        P(),
        P(),
    )
    out_specs = P(None, None, "loop", None, None)
    return jax.shard_map(local, mesh=mesh, in_specs=in_specs, out_specs=out_specs, check_vma=False)
```

profile of v0, /device:TPU:32, one launch (start us, length us, event | category | flops | bytes accessed | tf_op | source)
XLA Modules:
  0.0 1021.7 jit_solution(5908250101662363658)
XLA Ops:
  7.4 32.0 %while.56 = (s32[]{:T(128)}, f32[12,128]{1,0:T(8,128)S(1)}, f32[12,128]{1,0:T(8,128)S(1)}, f32[12,128,128]{2,1,0:T(8,128)S(1)}, pred[12,512]{1,0:T(8,128)(4,1)S(...) while((s32[]{:T(128)}, f32[12,128]{1,0:T(8,128)S(1)}, ...), condition=%wide.region_4.5_spmd, body=%wide.region_1.4_spmd.sunk | while | flops 34275072 | bytes 1155705 | solution.py:50
  7.5 1.3 select_reduce_fusion.9
  10.2 1.2 select_reduce_fusion.9
  12.9 1.2 select_reduce_fusion.9
  15.5 1.2 select_reduce_fusion.9
  26.2 1.2 select_reduce_fusion.9
  34.2 1.2 select_reduce_fusion.9
  40.1 1.3 select_reduce_fusion.4
  42.5 1.7 collective-permute-start
  44.9 31.7 %while.57 = (s32[]{:T(128)}, f32[12,128]{1,0:T(8,128)S(1)}, f32[12,128]{1,0:T(8,128)S(1)}, f32[12,128,128]{2,1,0:T(8,128)S(1)}, pred[12,512]{1,0:T(8,128)(4,1)S(...) while((s32[]{:T(128)}, f32[12,128]{1,0:T(8,128)S(1)}, ...), condition=%wide.region_8.9_spmd, body=%wide.region_5.8_spmd.sunk | while | flops 34275072 | bytes 1155705 | solution.py:50
  76.7 1.3 fusion.42
  78.0 1.6 collective-permute-start.12
  80.8 3.0 collective-permute-done.5
  83.9 31.7 %while.58 = (s32[]{:T(128)}, f32[12,128]{1,0:T(8,128)S(1)}, f32[12,128]{1,0:T(8,128)S(1)}, f32[12,128,128]{2,1,0:T(8,128)S(1)}, pred[12,512]{1,0:T(8,128)(4,1)S(...) while((s32[]{:T(128)}, f32[12,128]{1,0:T(8,128)S(1)}, ...), condition=%wide.region_12.13_spmd, body=%wide.region_9.12_spmd.sunk | while | flops 34275072 | bytes 1155705 | solution.py:50
  115.6 1.3 fusion.41
  117.0 1.7 collective-permute-start.13
  119.9 2.9 collective-permute-done.8
  122.9 31.7 %while.59 = (s32[]{:T(128)}, f32[12,128]{1,0:T(8,128)S(1)}, f32[12,128]{1,0:T(8,128)S(1)}, f32[12,128,128]{2,1,0:T(8,128)S(1)}, pred[12,512]{1,0:T(8,128)(4,1)S(...) while((s32[]{:T(128)}, f32[12,128]{1,0:T(8,128)S(1)}, ...), condition=%wide.region_16.17_spmd, body=%wide.region_13.16_spmd.sunk | while | flops 34275072 | bytes 1155705 | solution.py:50
  155.2 1.7 collective-permute-start.10
  156.9 9.7 collective-permute-done.10
  166.7 177.8 %pmax.7 = f32[1,12,128]{2,1,0:T(8,128)S(1)} all-reduce(f32[1,12,128]{2,1,0:T(8,128)S(1)} %collective-permute-done.10), channel_id=1, replica_groups=mesh['loop'=4,'grp'=64] {'grp'}, use_global_device_ids=true, to_apply=%region_17.18 | all-reduce | flops 1536 | bytes 12288 | tf_op jit(solution)/shard_map/pmax | solution.py:76
  345.7 178.5 %psum.15 = f32[12,128]{1,0:T(8,128)S(1)} all-reduce(f32[12,128]{1,0:T(8,128)S(1)} %get-tuple-element.268), channel_id=1, replica_groups=mesh['loop'=4,'grp'=64] {'grp'}, use_global_device_ids=true, to_apply=%region_20.21 | all-reduce | flops 1536 | bytes 12288 | tf_op jit(solution)/shard_map/psum | solution.py:78
  524.2 488.5 %all-reduce.2.cloned.1.call-done = f32[1,12,128,128]{3,2,1,0:T(8,128)} async-done(((f32[1,12,128,128]{3,2,1,0:T(8,128)}), f32[1,12,128,128]{3,2,1,0:T(8,128)}) %all-reduce.2.cloned.1.call-update) | async-done | bytes 786448 | tf_op jit(solution)/shard_map/psum | solution.py:78
  1012.7 2.2 divide_convert_fusion
  (340 shorter events, 126.3 us)
Async XLA Ops:
  6.5 35.0 %copy-start = (bf16[1,12,32,128]{3,2,1,0:T(8,128)(2,1)S(1)}, bf16[1,12,32,128]{3,2,1,0:T(8,128)(2,1)}, u32[]{:S(2)}) copy-start(bf16[1,12,32,128]{3,2,1,0:T(8,128)(2,1)} %param.19) | copy-start | bytes 294916
  6.5 1006.2 %all-reduce.2.cloned.1.call-start = ((), (), s32[]{:S(2)}) async-start(), calls=%async_computation | async-start | bytes 1572864 | tf_op jit(solution)/shard_map/psum | solution.py:78
  6.5 38.2 %collective-permute-start.2 = (bf16[1,12,128,128]{3,2,1,0:T(8,128)(2,1)}, bf16[1,12,128,128]{3,2,1,0:T(8,128)(2,1)S(1)}, u32[]{:S(2)}, u32[]{:S(2)}) collective-permute-start(bf16[1,12,128,128]{3,2,1,0:T(8,128)(2,1)} %bitcast.230), channel_id=1, source_target_pairs={{0,64},{64,128},{128,192},{192,0},{1,65},{65,129},{129,193},{193,1... | collective-permute-start | bytes 1179656 | tf_op jit(solution)/shard_map/ppermute | solution.py:13
  7.4 32.0 %copy-start.1 = (s32[12,32,32]{2,1,0:T(8,128)S(1)}, s32[12,32,32]{2,1,0:T(8,128)}, u32[]{:S(2)}) copy-start(s32[12,32,32]{2,1,0:T(8,128)} %param.20) | copy-start | bytes 147460
  7.4 32.7 %copy-start.2 = (bf16[1,12,32,128]{3,2,1,0:T(8,128)(2,1)S(1)}, bf16[1,12,32,128]{3,2,1,0:T(8,128)(2,1)}, u32[]{:S(2)}) copy-start(bf16[1,12,32,128]{3,2,1,0:T(8,128)(2,1)} %param.18) | copy-start | bytes 294916
  42.5 37.2 %collective-permute-start = (f32[1,12,128,128]{3,2,1,0:T(8,128)S(1)}, f32[1,12,128,128]{3,2,1,0:T(8,128)S(1)}, u32[]{:S(2)}, u32[]{:S(2)}) collective-permute-start(f32[1,12,128,128]{3,2,1,0:T(8,128)S(1)} %fusion.37), channel_id=1, source_target_pairs={{0,64},{64,128},{128,192},{192,0},{1,65},{65,129},{129,193},{193,1... | collective-permute-start | bytes 2359304 | tf_op jit(solution)/shard_map/ppermute | solution.py:13
  44.2 32.5 %collective-permute-start.11 = (f32[1,12,128]{2,1,0:T(8,128)S(1)}, f32[1,12,128]{2,1,0:T(8,128)}, u32[]{:S(2)}, u32[]{:S(2)}) collective-permute-start(f32[1,12,128]{2,1,0:T(8,128)S(1)} %get-tuple-element.257), channel_id=1, source_target_pairs={{0,64},{64,128},{128,192},{192,0},{1,65},{65,129},{129,193},{193,1... | collective-permute-start | bytes 18440 | tf_op jit(solution)/shard_map/ppermute | solution.py:13
  44.3 32.4 %collective-permute-start.1 = (f32[1,12,128]{2,1,0:T(8,128)S(1)}, f32[1,12,128]{2,1,0:T(8,128)}, u32[]{:S(2)}, u32[]{:S(2)}) collective-permute-start(f32[1,12,128]{2,1,0:T(8,128)S(1)} %get-tuple-element.282), channel_id=1, source_target_pairs={{0,64},{64,128},{128,192},{192,0},{1,65},{65,129},{129,193},{193,1... | collective-permute-start | bytes 18440 | tf_op jit(solution)/shard_map/ppermute | solution.py:13
  76.5 7.3 collective-permute-start.5
  78.0 37.6 %collective-permute-start.12 = (f32[1,12,128]{2,1,0:T(8,128)}, f32[1,12,128]{2,1,0:T(8,128)S(1)}, u32[]{:S(2)}, u32[]{:S(2)}) collective-permute-start(f32[1,12,128]{2,1,0:T(8,128)} %get-tuple-element.278), channel_id=1, source_target_pairs={{0,64},{64,128},{128,192},{192,0},{1,65},{65,129},{129,193},{193,1... | collective-permute-start | bytes 18440 | tf_op jit(solution)/shard_map/ppermute | solution.py:13
  79.6 36.0 %collective-permute-start.4 = (f32[1,12,128]{2,1,0:T(8,128)S(1)}, f32[1,12,128]{2,1,0:T(8,128)}, u32[]{:S(2)}, u32[]{:S(2)}) collective-permute-start(f32[1,12,128]{2,1,0:T(8,128)S(1)} %get-tuple-element.281), channel_id=1, source_target_pairs={{0,64},{64,128},{128,192},{192,0},{1,65},{65,129},{129,193},{193,1... | collective-permute-start | bytes 18440 | tf_op jit(solution)/shard_map/ppermute | solution.py:13
  80.2 38.5 %collective-permute-start.3 = (f32[1,12,128,128]{3,2,1,0:T(8,128)S(1)}, f32[1,12,128,128]{3,2,1,0:T(8,128)S(1)}, u32[]{:S(2)}, u32[]{:S(2)}) collective-permute-start(f32[1,12,128,128]{3,2,1,0:T(8,128)S(1)} %bitcast_add_fusion.2), channel_id=1, source_target_pairs={{0,64},{64,128},{128,192},{192,0},{1,65},{65,129},{129,193},{193,1... | collective-permute-start | bytes 2359304 | tf_op jit(solution)/shard_map/ppermute | solution.py:13
  115.5 7.3 collective-permute-start.8
  117.0 37.6 %collective-permute-start.13 = (f32[1,12,128]{2,1,0:T(8,128)}, f32[1,12,128]{2,1,0:T(8,128)S(1)}, u32[]{:S(2)}, u32[]{:S(2)}) collective-permute-start(f32[1,12,128]{2,1,0:T(8,128)} %get-tuple-element.274), channel_id=1, source_target_pairs={{0,64},{64,128},{128,192},{192,0},{1,65},{65,129},{129,193},{193,1... | collective-permute-start | bytes 18440 | tf_op jit(solution)/shard_map/ppermute | solution.py:13
  118.6 35.9 %collective-permute-start.7 = (f32[1,12,128]{2,1,0:T(8,128)S(1)}, f32[1,12,128]{2,1,0:T(8,128)S(1)}, u32[]{:S(2)}, u32[]{:S(2)}) collective-permute-start(f32[1,12,128]{2,1,0:T(8,128)S(1)} %get-tuple-element.277), channel_id=1, source_target_pairs={{0,64},{64,128},{128,192},{192,0},{1,65},{65,129},{129,193},{193,1... | collective-permute-start | bytes 18440 | tf_op jit(solution)/shard_map/ppermute | solution.py:13
  119.1 35.5 %collective-permute-start.6 = (f32[1,12,128,128]{3,2,1,0:T(8,128)S(1)}, f32[1,12,128,128]{3,2,1,0:T(8,128)S(1)}, u32[]{:S(2)}, u32[]{:S(2)}) collective-permute-start(f32[1,12,128,128]{3,2,1,0:T(8,128)S(1)} %bitcast_add_fusion.1), channel_id=1, source_target_pairs={{0,64},{64,128},{128,192},{192,0},{1,65},{65,129},{129,193},{193,1... | collective-permute-start | bytes 2359304 | tf_op jit(solution)/shard_map/ppermute | solution.py:13
  155.1 189.4 %collective-permute-start.9 = (f32[1,12,128,128]{3,2,1,0:T(8,128)S(1)}, f32[1,12,128,128]{3,2,1,0:T(8,128)S(1)}, u32[]{:S(2)}, u32[]{:S(2)}) collective-permute-start(f32[1,12,128,128]{3,2,1,0:T(8,128)S(1)} %bitcast_add_fusion), channel_id=1, source_target_pairs={{0,64},{64,128},{128,192},{192,0},{1,65},{65,129},{129,193},{193,1... | collective-permute-start | bytes 2359304 | tf_op jit(solution)/shard_map/ppermute | solution.py:13
  155.2 11.5 %collective-permute-start.10 = (f32[1,12,128]{2,1,0:T(8,128)S(1)}, f32[1,12,128]{2,1,0:T(8,128)S(1)}, u32[]{:S(2)}, u32[]{:S(2)}) collective-permute-start(f32[1,12,128]{2,1,0:T(8,128)S(1)} %get-tuple-element.273), channel_id=1, source_target_pairs={{0,64},{64,128},{128,192},{192,0},{1,65},{65,129},{129,193},{193,1... | collective-permute-start | bytes 18440 | tf_op jit(solution)/shard_map/ppermute | solution.py:13
  156.9 187.6 %collective-permute-start.14 = (f32[1,12,128]{2,1,0:T(8,128)S(1)}, f32[1,12,128]{2,1,0:T(8,128)S(1)}, u32[]{:S(2)}, u32[]{:S(2)}) collective-permute-start(f32[1,12,128]{2,1,0:T(8,128)S(1)} %get-tuple-element.270), channel_id=1, source_target_pairs={{0,64},{64,128},{128,192},{192,0},{1,65},{65,129},{129,193},{193,1... | collective-permute-start | bytes 18440 | tf_op jit(solution)/shard_map/ppermute | solution.py:13
Sparse Core Ops, SparseCore 0:
  345.8 666.8 all-reduce.1
where the time goes:
time: 1030 us; the launch traced here: 1020 us
  waiting for transfers between devices  504 us (49%)
  blocking collectives  356 us (35%)
  matrix products  114 us (11%)
  other arithmetic  17.4 us (2%)
  between operations  13.7 us (1%)
    psum x1, waiting for transfers between devices, group_reduce(): lax.psum((partial_value[1] * factor, partial_value[2] * factor[..., None]...  488 us
    psum x1, blocking collectives, group_reduce(): lax.psum((partial_value[1] * factor, partial_value[2] * factor[..., None]...  179 us
    pmax x1, blocking collectives, group_reduce(): peak = lax.pmax(partial_value[0], 'grp')  178 us
    dot_general x48, matrix products, one_sequence(): lax.dot_general(query_block, key_block, (((1,), (1,)), ((), ())), preferr...  56.7 us
    dot_general x48, matrix products, one_sequence(): summed = jnp.dot(weights, value_block, preferred_element_type=jnp.float32)  55.1 us
  transfers between devices with their start and end apart: 16, of which 4 were waited for; matrix products, arithmetic and copies ran while one was open for 13% of the time, Pallas kernels for 0%

commit v1 on v0

v1 whole, which is shorter than its diff:
```python
import functools
import math

import jax
import jax.numpy as jnp
from jax import lax
from jax.experimental import pallas as pl
from jax.experimental.pallas import tpu as pltpu
from jax.sharding import PartitionSpec as P

MESH = pl.DeviceIdType.MESH
F32 = jnp.float32
BF16 = jnp.bfloat16

SEQS = 12
ROWS = 128
KEYS = 512
WIDTH = 128
DRAFT = 32
NX, NY, NZ = 4, 4, 8
CHUNKS = 3
PER = SEQS // CHUNKS
PIECE = 16
SPAN = PER * PIECE
SLICE = SPAN // NZ
NEAR = [(dx, dy) for dy in (0, 2) for dx in range(NX) if (dx, dy) != (0, 0)]
FAR = [(dx, dy) for dy in (1, 3) for dx in range(NX)]
PLANE = NEAR + FAR

SCALE = math.log2(math.e) / math.sqrt(WIDTH)
FLOOR = -1e30
LOW = -1e29


def iota(shape, axis):
    return lax.broadcasted_iota(jnp.int32, shape, axis)


def to_row(column):
    eye = iota((ROWS, ROWS), 0) == iota((ROWS, ROWS), 1)
    return jnp.sum(jnp.where(eye, column, 0.0), axis=0, keepdims=True)


def to_column(row, rows, first):
    pick = iota((rows, ROWS), 1) == iota((rows, ROWS), 0) + first
    return jnp.sum(jnp.where(pick, row, 0.0), axis=1, keepdims=True)


def by_piece(tile):
    lane = iota((8, ROWS), 1) // PIECE
    sub = iota((8, ROWS), 0)
    out = jnp.zeros((8, ROWS), F32)
    for d in range(8):
        moved = tile if d == 0 else pltpu.roll(tile, PIECE * d, 1)
        diagonal = jnp.sum(jnp.where(lane == sub, moved, 0.0), axis=0, keepdims=True)
        out = jnp.where((lane - sub + 8) % 8 == d, diagonal, out)
    return out


def kernel(
    q_hbm, k_hbm, v_hbm, dk_hbm, dv_hbm, tm_hbm, vl_hbm, out_ref,
    Q, K, V, DK, DV, TM, VL,
    own, own_s, give, give_s, got, got_s,
    plane, plane_s, land, land_s,
    zed, zed_s, zland, zland_s, done,
    ld, ld_small, q_send, q_recv, c_send, c_recv, a_send, a_recv, z_send, z_recv, g_send, g_recv, o_send, o_recv,
):
    loop_index = lax.axis_index("loop")
    group_index = lax.axis_index("grp")
    core = loop_index % 2
    x = group_index % NX
    z = (group_index // NX) % NZ
    y = (group_index // (NX * NZ)) * 2 + loop_index // 2

    def device(px, py, pz, pc):
        return ((py % 2) * 2 + pc, ((py // 2) * NZ + pz) * NX + px)

    mate = device(x, y, z, 1 - core)

    def in_plane(dx, dy):
        return device((x + dx) % NX, (y + dy) % NY, z, core)

    def along_z(dz):
        return device(x, y, (z + dz) % NZ, core)

    def piece_of(px, py):
        return (py // 2) * NX + px

    mine = piece_of(x, y)

    def remote(src, dst, send, recv, target):
        return pltpu.make_async_remote_copy(
            src_ref=src, dst_ref=dst, send_sem=send, recv_sem=recv, device_id=target, device_id_type=MESH
        )

    peers = [mate] + [in_plane(dx, dy) for dx, dy in PLANE] + [along_z(dz) for dz in range(1, NZ)]
    barrier = pltpu.get_barrier_semaphore()
    for peer in peers:
        pl.semaphore_signal(barrier, inc=1, device_id=peer, device_id_type=MESH)

    def seqs(c):
        return pl.ds(c * PER, PER)

    def load(c):
        return [
            pltpu.make_async_copy(q_hbm.at[seqs(c)], Q.at[0, seqs(c)], ld.at[c, 0]),
            pltpu.make_async_copy(k_hbm.at[seqs(c)], K.at[seqs(c)], ld.at[c, 1]),
            pltpu.make_async_copy(v_hbm.at[seqs(c)], V.at[seqs(c)], ld.at[c, 2]),
        ]

    small = [
        pltpu.make_async_copy(vl_hbm, VL, ld_small.at[0]),
        pltpu.make_async_copy(dk_hbm, DK, ld_small.at[1]),
        pltpu.make_async_copy(dv_hbm, DV, ld_small.at[2]),
        pltpu.make_async_copy(tm_hbm, TM, ld_small.at[3]),
    ]
    small[0].start()
    for c in range(CHUNKS):
        for copy in load(c):
            copy.start()
    for copy in small[1:]:
        copy.start()

    half = ROWS // 2

    def ask_mate(c):
        return remote(q_hbm.at[seqs(c)], Q.at[1, seqs(c)], q_send.at[c, 0], q_recv.at[c, 0], mate)

    def ask_far(c, side):
        rows = pl.ds(side * half, half)
        return remote(
            q_hbm.at[seqs(c), rows], Q.at[2, seqs(c), rows], q_send.at[c, 1 + side], q_recv.at[c, 1 + side],
            in_plane(0, 1 if side == 0 else 3),
        )

    def pass_on(c):
        return remote(Q.at[2, seqs(c)], Q.at[3, seqs(c)], q_send.at[c, 3], q_recv.at[c, 3], mate)

    first = (loop_index * (NX * 2 * NZ) + group_index) * KEYS
    position = first + iota((1, KEYS), 1)
    ones = jnp.ones((KEYS, WIDTH), BF16)
    sub8 = iota((8, ROWS), 0)

    def attend(j, c, sums, figures, side):
        def one(i, tile):
            s = c * PER + i
            scores = lax.dot_general(Q[j, s], K[s], (((1,), (1,)), ((), ())), preferred_element_type=F32)
            scores = jnp.where(position < VL[s], scores * SCALE, FLOOR)
            peak = jnp.maximum(jnp.max(scores, axis=1, keepdims=True), LOW)
            weights = jnp.exp2(scores - peak).astype(BF16)
            both = jnp.dot(weights, jnp.concatenate([V[s], ones], axis=1), preferred_element_type=F32)
            sums[side, s] = both[:, :WIDTH].astype(sums.dtype)
            tile = jnp.where(sub8 == i, to_row(peak), tile)
            return jnp.where(sub8 == PER + i, to_row(both[:, WIDTH:]), tile)

        figures[side, c] = lax.fori_loop(0, PER, one, jnp.zeros((8, ROWS), F32))

    def swap(side, c):
        return [
            remote(give.at[side, seqs(c)], got.at[side, seqs(c)], c_send.at[side, c, 0], c_recv.at[side, c, 0], mate),
            remote(give_s.at[side, c], got_s.at[side, c], c_send.at[side, c, 1], c_recv.at[side, c, 1], mate),
        ]

    def merge_cores(side, c):
        for copy in swap(side, c):
            copy.wait_recv()
        a, b = own_s[side, c], got_s[side, c]
        is_peak = sub8 < PER
        joined = jnp.maximum(a, b)
        fa = jnp.exp2(jnp.where(is_peak, a - joined, 0.0))
        fb = jnp.exp2(jnp.where(is_peak, b - joined, 0.0))
        total = pltpu.roll(fa, PER, 0) * a + pltpu.roll(fb, PER, 0) * b
        pieces = by_piece(jnp.where(is_peak, joined, total))
        for p in range(8):
            plane_s[side, c, p] = pieces[p : p + 1]

        for i in range(PER):
            s = c * PER + i
            plane[side, s] = (
                own[side, s] * to_column(fa[i : i + 1], ROWS, 0)
                + got[side, s].astype(F32) * to_column(fb[i : i + 1], ROWS, 0)
            ).astype(BF16)

    def scatter(side, c):
        copies = []
        for n, (dx, dy) in enumerate(PLANE):
            if (dy % 2) != side:
                continue
            piece = piece_of((x + dx) % NX, (y + dy) % NY)
            rows = pl.ds(pl.multiple_of(piece * PIECE, PIECE), PIECE)
            target = in_plane(dx, dy)
            copies.append(remote(plane.at[side, seqs(c), rows], land.at[c, n], a_send.at[c, n, 0], a_recv.at[c, n, 0], target))
            copies.append(remote(plane_s.at[side, c, piece], land_s.at[c, n], a_send.at[c, n, 1], a_recv.at[c, n, 1], target))
        return copies

    def merge_plane(c):
        for side in range(2):
            for copy in scatter(side, c):
                copy.wait_recv()
        figures = jnp.concatenate([plane_s[0, c, mine]] + [land_s[c, n] for n in range(len(PLANE))], axis=0)
        peak = jnp.max(figures, axis=0, keepdims=True)
        is_peak = iota((1, ROWS), 1) < SPAN
        factor = jnp.exp2(jnp.where(is_peak, figures - peak, 0.0))
        total = jnp.sum(pltpu.roll(factor, SPAN, 1) * figures, axis=0, keepdims=True)
        zed_s[c] = jnp.where(is_peak, peak, total)
        rows = pl.ds(pl.multiple_of(mine * PIECE, PIECE), PIECE)
        acc = plane[0, seqs(c), rows].reshape(SPAN, WIDTH).astype(F32) * to_column(factor[0:1], SPAN, 0)
        for n in range(len(PLANE)):
            acc += land[c, n].reshape(SPAN, WIDTH).astype(F32) * to_column(factor[n + 1 : n + 2], SPAN, 0)
        zed[c] = acc.reshape(NZ, SLICE, WIDTH)

    def spread(c):
        copies = []
        for dz in range(1, NZ):
            target = along_z(dz)
            copies.append(remote(zed.at[c, (z + dz) % NZ], zland.at[c, dz - 1], z_send.at[c, dz, 0], z_recv.at[c, dz, 0], target))
            copies.append(remote(zed_s.at[c], zland_s.at[c, dz - 1], z_send.at[c, dz, 1], z_recv.at[c, dz, 1], target))
        return copies

    def draft(c):
        s = c * PER + z // 2
        rows = pl.ds(pl.multiple_of(mine * PIECE, PIECE), PIECE)
        scores = lax.dot_general(Q[0, s, rows], DK[s], (((1,), (1,)), ((), ())), preferred_element_type=F32) * SCALE
        allowed = TM[s, pl.ds(pl.multiple_of((mine % 2) * PIECE, PIECE), PIECE)] == 1
        peak = jnp.max(jnp.where(allowed, scores, FLOOR), axis=1, keepdims=True)
        weights = jnp.where(allowed, jnp.exp2(scores - peak), 0.0).astype(BF16)
        total = jnp.sum(weights.astype(F32), axis=1, keepdims=True)
        sums = jnp.dot(weights, DV[s], preferred_element_type=F32)
        low = z % 2 == 0
        return tuple(jnp.where(low, a[:SLICE], a[SLICE:]) for a in (peak, total, sums))

    def finish(c, drafted):
        for copy in spread(c):
            copy.wait_recv()
        figures = jnp.concatenate([zed_s[c]] + [zland_s[c, n] for n in range(NZ - 1)], axis=0)
        peak = jnp.max(figures, axis=0, keepdims=True)
        is_peak = iota((1, ROWS), 1) < SPAN
        factor = jnp.exp2(jnp.where(is_peak, figures - peak, 0.0))
        total = jnp.sum(pltpu.roll(factor, SPAN, 1) * figures, axis=0, keepdims=True)
        here = z * SLICE
        acc = zed[c, z] * to_column(factor[0:1], SLICE, here)
        for n in range(NZ - 1):
            acc += zland[c, n] * to_column(factor[n + 1 : n + 2], SLICE, here)
        top = to_column(peak, SLICE, here)
        tot = to_column(total, SLICE, here + SPAN)
        d_top, d_tot, d_acc = drafted
        joined = jnp.maximum(top, d_top)
        fa, fb = jnp.exp2(top - joined), jnp.exp2(d_top - joined)
        done[c, z] = (acc * fa + d_acc * fb) / (tot * fa + d_tot * fb)

    def regather(c):
        return [
            remote(done.at[c, z], done.at[c, z], g_send.at[c, dz], g_recv.at[c, dz], along_z(dz)) for dz in range(1, NZ)
        ]

    def regathered(c):
        for dz in range(1, NZ):
            source = (z + NZ - dz) % NZ
            remote(done.at[c, z], done.at[c, source], g_send.at[c, dz], g_recv.at[c, dz], along_z(dz)).wait_recv()

    def deliver(c):
        rows = pl.ds(pl.multiple_of(mine * PIECE, PIECE), PIECE)
        part = out_ref.at[seqs(c), rows]
        return [
            remote(part, part, o_send.at[c, n], o_recv.at[c, n], in_plane(dx, dy)) for n, (dx, dy) in enumerate(NEAR)
        ]

    def delivered(c):
        rows = pl.ds(pl.multiple_of(mine * PIECE, PIECE), PIECE)
        for n, (dx, dy) in enumerate(NEAR):
            source = piece_of((x + NX - dx) % NX, (y + NY - dy) % NY)
            there = pl.ds(pl.multiple_of(source * PIECE, PIECE), PIECE)
            remote(
                out_ref.at[seqs(c), rows], out_ref.at[seqs(c), there], o_send.at[c, n], o_recv.at[c, n], in_plane(dx, dy)
            ).wait_recv()

    def start(copies):
        for copy in copies:
            copy.start()

    pl.semaphore_wait(barrier, len(peers))
    for c in range(CHUNKS):
        for side in range(2):
            ask_far(c, side).start()
    for c in range(CHUNKS):
        ask_mate(c).start()

    small[0].wait()

    def near_own(c, carry):
        for copy in load(c):
            copy.wait()
        attend(0, c, own, own_s, 0)
        return carry

    def near_mate(c, carry):
        ask_mate(c).wait_recv()
        attend(1, c, give, give_s, 0)
        start(swap(0, c))
        return carry

    def near_merge(c, carry):
        merge_cores(0, c)
        start(scatter(0, c))
        return carry

    def far_own(c):
        for side in range(2):
            ask_far(c, side).wait_recv()
        pass_on(c).start()
        attend(2, c, own, own_s, 1)

    def far_mate(c):
        pass_on(c).wait_recv()
        attend(3, c, give, give_s, 1)
        start(swap(1, c))

    def far_merge(c):
        merge_cores(1, c)
        start(scatter(1, c))

    lax.fori_loop(0, CHUNKS, near_own, 0)
    lax.fori_loop(0, CHUNKS, near_mate, 0)
    lax.fori_loop(0, CHUNKS, near_merge, 0)

    def far(c, carry):
        far_own(c)
        far_mate(c)
        return carry

    def far2(c, carry):
        far_merge(c)
        return carry

    lax.fori_loop(0, CHUNKS, far, 0)
    lax.fori_loop(0, CHUNKS, far2, 0)

    for copy in small[1:]:
        copy.wait()
    drafted = [draft(c) for c in range(CHUNKS)]

    for c in range(CHUNKS):
        merge_plane(c)
        start(spread(c))
    for c in range(CHUNKS):
        finish(c, drafted[c])
        start(regather(c))
    for c in range(CHUNKS):
        regathered(c)
        rows = pl.ds(pl.multiple_of(mine * PIECE, PIECE), PIECE)
        out_ref[seqs(c), rows] = done[c].reshape(PER, PIECE, WIDTH).astype(BF16)
        start(deliver(c))

    for c in range(CHUNKS):
        sent = [ask_mate(c), ask_far(c, 0), ask_far(c, 1), pass_on(c)]
        sent += swap(0, c) + swap(1, c) + scatter(0, c) + scatter(1, c) + spread(c) + regather(c) + deliver(c)
        for copy in sent:
            copy.wait_send()
        delivered(c)


def local(queries, cache_keys, cache_values, draft_keys, draft_values, tree_mask, valid_length):
    dma = pltpu.SemaphoreType.DMA
    n = len(PLANE)
    scratch = [
        pltpu.VMEM((4, SEQS, ROWS, WIDTH), BF16),
        pltpu.VMEM((SEQS, KEYS, WIDTH), BF16),
        pltpu.VMEM((SEQS, KEYS, WIDTH), BF16),
        pltpu.VMEM((SEQS, DRAFT, WIDTH), BF16),
        pltpu.VMEM((SEQS, DRAFT, WIDTH), BF16),
        pltpu.VMEM((SEQS, DRAFT, DRAFT), jnp.int32),
        pltpu.SMEM((SEQS,), jnp.int32),
        pltpu.VMEM((2, SEQS, ROWS, WIDTH), F32),
        pltpu.VMEM((2, CHUNKS, 8, ROWS), F32),
        pltpu.VMEM((2, SEQS, ROWS, WIDTH), BF16),
        pltpu.VMEM((2, CHUNKS, 8, ROWS), F32),
        pltpu.VMEM((2, SEQS, ROWS, WIDTH), BF16),
        pltpu.VMEM((2, CHUNKS, 8, ROWS), F32),
        pltpu.VMEM((2, SEQS, ROWS, WIDTH), BF16),
        pltpu.VMEM((2, CHUNKS, 8, 1, ROWS), F32),
        pltpu.VMEM((CHUNKS, n, PER, PIECE, WIDTH), BF16),
        pltpu.VMEM((CHUNKS, n, 1, ROWS), F32),
        pltpu.VMEM((CHUNKS, NZ, SLICE, WIDTH), F32),
        pltpu.VMEM((CHUNKS, 1, ROWS), F32),
        pltpu.VMEM((CHUNKS, NZ - 1, SLICE, WIDTH), F32),
        pltpu.VMEM((CHUNKS, NZ - 1, 1, ROWS), F32),
        pltpu.VMEM((CHUNKS, NZ, SLICE, WIDTH), F32),
        dma((CHUNKS, 3)),
        dma((4,)),
        dma((CHUNKS, 4)),
        dma((CHUNKS, 4)),
        dma((2, CHUNKS, 2)),
        dma((2, CHUNKS, 2)),
        dma((CHUNKS, n, 2)),
        dma((CHUNKS, n, 2)),
        dma((CHUNKS, NZ, 2)),
        dma((CHUNKS, NZ, 2)),
        dma((CHUNKS, NZ)),
        dma((CHUNKS, NZ)),
        dma((CHUNKS, len(NEAR))),
        dma((CHUNKS, len(NEAR))),
    ]
    out = pl.pallas_call(
        kernel,
        out_shape=jax.ShapeDtypeStruct((SEQS, ROWS, WIDTH), BF16),
        in_specs=[pl.BlockSpec(memory_space=pltpu.HBM)] * 7,
        out_specs=pl.BlockSpec(memory_space=pltpu.VMEM),
        scratch_shapes=scratch,
        compiler_params=pltpu.CompilerParams(collective_id=0, has_side_effects=True, vmem_limit_bytes=48 << 20),
        name="attend",
    )(
        queries.reshape(SEQS, ROWS, WIDTH),
        cache_keys.reshape(SEQS, KEYS, WIDTH),
        cache_values.reshape(SEQS, KEYS, WIDTH),
        draft_keys.reshape(SEQS, DRAFT, WIDTH),
        draft_values.reshape(SEQS, DRAFT, WIDTH),
        tree_mask,
        valid_length,
    )
    return out.reshape(queries.shape)


def solution(mesh):
    in_specs = (
        P(None, None, "loop", None, None),
        P(None, None, ("loop", "grp"), None),
        P(None, None, ("loop", "grp"), None),
        P(),
        P(),
        P(),
        P(),
    )
    out_specs = P(None, None, "loop", None, None)
    return jax.shard_map(local, mesh=mesh, in_specs=in_specs, out_specs=out_specs, check_vma=False)
```

time: 1030 us -> 68.2 us (0.07)
  waiting for transfers between devices: 504 us -> 0 us
  blocking collectives: 356 us -> 0 us
  matrix products: 114 us -> 0 us
  Pallas kernels: 0 us -> 59.4 us
  other arithmetic: 17.4 us -> 0 us
  between operations: 13.7 us -> 0.02 us
    psum x1 -> x0, waiting for transfers between devices: 488 us -> none  [group_reduce(): lax.psum((partial_value[1] * factor, partial_value[2] * factor[..., None]...]
    psum x1 -> x0, blocking collectives: 179 us -> none  [group_reduce(): lax.psum((partial_value[1] * factor, partial_value[2] * factor[..., None]...]
    pmax x1 -> x0, blocking collectives: 178 us -> none  [group_reduce(): peak = lax.pmax(partial_value[0], 'grp')]
    dot_general x98 -> x0, matrix products: 114 us -> none  [the longest x48 56.7 us: one_sequence(): lax.dot_general(query_block, key_block, (((1,), (1,)), ((), ())), preferr...]
    pallas_call x0 -> x1, Pallas kernels: none -> 59.4 us  [local(): pl.pallas_call(kernel, out_shape=jax.ShapeDtypeStruct((SEQS, ROWS, WIDTH)...]
    ppermute x15 -> x0, waiting for transfers between devices: 15.7 us -> none  [from_behind(): lax.ppermute(shard, axis, [(i, (i + by) % count) for i in range(count)])]
  transfers between devices with their start and end apart: 16 -> 0, of which waited for: 4 -> 0; matrix products, arithmetic and copies ran while one was open for 13% -> 0% of each run, Pallas kernels for 0% -> 0%
where the time goes in v1:
time: 68.2 us; the launch traced here: 67.3 us
  Pallas kernels  59.4 us (87%)
  local copies, waits for them, and re-layouts  7.92 us (12%)
    pallas_call x1, Pallas kernels, local(): pl.pallas_call(kernel, out_shape=jax.ShapeDtypeStruct((SEQS, ROWS, WIDTH)...  59.4 us
    unnamed x15, local copies, waits for them, and re-layouts  7.92 us

profile of v1, /device:TPU:32, one launch (start us, length us, event | category | flops | bytes accessed | tf_op | source)
XLA Modules:
  0.0 67.3 jit_solution(6794890582128577625)
XLA Ops:
  0.0 0.0 copy-start
  0.0 1.4 %copy-done = bf16[1,12,512,128]{3,2,1,0:T(8,128)(2,1)S(1)} copy-done((bf16[1,12,512,128]{3,2,1,0:T(8,128)(2,1)S(1)}, bf16[1,12,512,128]{3,2,1,0:T(8,128)(2,1)}, u32[]{:S(2)}) %copy-start) | copy-done | bytes 1572888
  1.4 0.0 copy-start.1
  1.4 1.4 %copy-done.1 = bf16[1,12,512,128]{3,2,1,0:T(8,128)(2,1)S(1)} copy-done((bf16[1,12,512,128]{3,2,1,0:T(8,128)(2,1)S(1)}, bf16[1,12,512,128]{3,2,1,0:T(8,128)(2,1)}, u32[]{:S(2)}) %copy-start.1) | copy-done | bytes 1572888
  2.8 0.0 copy-start.2
  2.8 1.0 %copy-done.2 = bf16[1,12,4,32,128]{4,3,2,1,0:T(8,128)(2,1)S(1)} copy-done((bf16[1,12,4,32,128]{4,3,2,1,0:T(8,128)(2,1)S(1)}, bf16[1,12,4,32,128]{4,3,2,1,0:T(8,128)(2,1)}, u32[]{:S(2)}) %copy-start.2) | copy-done | bytes 393240
  3.8 0.0 copy-start.3
  3.8 0.9 %copy-done.3 = s32[12,32,32]{2,1,0:T(8,128)S(1)} copy-done((s32[12,32,32]{2,1,0:T(8,128)S(1)}, s32[12,32,32]{2,1,0:T(8,128)}, u32[]{:S(2)}) %copy-start.3) | copy-done | bytes 49176
  4.7 0.0 copy-start.4
  4.7 0.9 %copy-done.4 = bf16[1,12,32,128]{3,2,1,0:T(8,128)(2,1)S(1)} copy-done((bf16[1,12,32,128]{3,2,1,0:T(8,128)(2,1)S(1)}, bf16[1,12,32,128]{3,2,1,0:T(8,128)(2,1)}, u32[]{:S(2)}) %copy-start.4) | copy-done | bytes 98328
  5.6 0.0 copy-start.5
  5.6 0.9 %copy-done.5 = bf16[1,12,32,128]{3,2,1,0:T(8,128)(2,1)S(1)} copy-done((bf16[1,12,32,128]{3,2,1,0:T(8,128)(2,1)S(1)}, bf16[1,12,32,128]{3,2,1,0:T(8,128)(2,1)}, u32[]{:S(2)}) %copy-start.5) | copy-done | bytes 98328
  6.5 0.0 copy-start.6
  6.5 0.7 copy-done.6
  7.2 59.4 %attend.1 = bf16[12,128,128]{2,1,0:T(8,128)(2,1)S(1)} custom-call(bf16[12,128,128]{2,1,0:T(8,128)(2,1)S(1)} %bitcast.9, bf16[12,512,128]{2,1,0:T(8,128)(2,1)S(1)} %bitcast.6, bf16[12,512,128]{2,1,0:T(8,128)(2,1)S(1)} %bitcast.7, bf16[12,32,128]{2,1,0:T(8,128)(2,1)S(1)} %bitcast.10, bf16[12,32,128]{2,1,0:T(8,128)(2,1)S(1)} %bitcast.11, ...), custom_call_target="tpu_custom_call" | custom-call | tf_op jit(solution)/shard_map/attend/pallas_call | solution.py:403
  66.6 0.7 %copy.9 = bf16[1,12,4,32,128]{4,3,2,1,0:T(8,128)(2,1)} copy(bf16[1,12,4,32,128]{4,3,2,1,0:T(8,128)(2,1)S(1)} %bitcast.8) | data formatting | bytes 786432
Async XLA Ops:
  0.0 1.4 %copy-start = (bf16[1,12,512,128]{3,2,1,0:T(8,128)(2,1)S(1)}, bf16[1,12,512,128]{3,2,1,0:T(8,128)(2,1)}, u32[]{:S(2)}) copy-start(bf16[1,12,512,128]{3,2,1,0:T(8,128)(2,1)} %param.8) | copy-start | bytes 4718596
  1.4 1.4 %copy-start.1 = (bf16[1,12,512,128]{3,2,1,0:T(8,128)(2,1)S(1)}, bf16[1,12,512,128]{3,2,1,0:T(8,128)(2,1)}, u32[]{:S(2)}) copy-start(bf16[1,12,512,128]{3,2,1,0:T(8,128)(2,1)} %param.9) | copy-start | bytes 4718596
  2.8 1.0 %copy-start.2 = (bf16[1,12,4,32,128]{4,3,2,1,0:T(8,128)(2,1)S(1)}, bf16[1,12,4,32,128]{4,3,2,1,0:T(8,128)(2,1)}, u32[]{:S(2)}) copy-start(bf16[1,12,4,32,128]{4,3,2,1,0:T(8,128)(2,1)} %param.7) | copy-start | bytes 1179652
  3.8 0.9 %copy-start.3 = (s32[12,32,32]{2,1,0:T(8,128)S(1)}, s32[12,32,32]{2,1,0:T(8,128)}, u32[]{:S(2)}) copy-start(s32[12,32,32]{2,1,0:T(8,128)} %tm_hbm.1) | copy-start | bytes 147460
  4.7 0.9 %copy-start.4 = (bf16[1,12,32,128]{3,2,1,0:T(8,128)(2,1)S(1)}, bf16[1,12,32,128]{3,2,1,0:T(8,128)(2,1)}, u32[]{:S(2)}) copy-start(bf16[1,12,32,128]{3,2,1,0:T(8,128)(2,1)} %param.10) | copy-start | bytes 294916
  5.6 0.9 %copy-start.5 = (bf16[1,12,32,128]{3,2,1,0:T(8,128)(2,1)S(1)}, bf16[1,12,32,128]{3,2,1,0:T(8,128)(2,1)}, u32[]{:S(2)}) copy-start(bf16[1,12,32,128]{3,2,1,0:T(8,128)(2,1)} %param.11) | copy-start | bytes 294916
  6.5 0.7 copy-start.6

commit v2 on v1

--- a/solution.py
+++ b/solution.py
@@ -124,17 +124,20 @@
     half = ROWS // 2
 
     def ask_mate(c):
-        return remote(q_hbm.at[seqs(c)], Q.at[1, seqs(c)], q_send.at[c, 0], q_recv.at[c, 0], mate)
+        return remote(q_hbm.at[seqs(c)], Q.at[1, seqs(c)], q_send.at[0], q_recv.at[0, c], mate)
 
     def ask_far(c, side):
         rows = pl.ds(side * half, half)
         return remote(
-            q_hbm.at[seqs(c), rows], Q.at[2, seqs(c), rows], q_send.at[c, 1 + side], q_recv.at[c, 1 + side],
+            q_hbm.at[seqs(c), rows], Q.at[2, seqs(c), rows], q_send.at[1], q_recv.at[1, c],
             in_plane(0, 1 if side == 0 else 3),
         )
 
     def pass_on(c):
-        return remote(Q.at[2, seqs(c)], Q.at[3, seqs(c)], q_send.at[c, 3], q_recv.at[c, 3], mate)
+        return remote(Q.at[2, seqs(c)], Q.at[3, seqs(c)], q_send.at[2], q_recv.at[2, c], mate)
+
+    def await_far(c):
+        remote(Q.at[2, seqs(c)], Q.at[2, seqs(c)], q_send.at[1], q_recv.at[1, c], mate).wait_recv()
 
     first = (loop_index * (NX * 2 * NZ) + group_index) * KEYS
     position = first + iota((1, KEYS), 1)
@@ -153,12 +156,12 @@
             tile = jnp.where(sub8 == i, to_row(peak), tile)
             return jnp.where(sub8 == PER + i, to_row(both[:, WIDTH:]), tile)
 
-        figures[side, c] = lax.fori_loop(0, PER, one, jnp.zeros((8, ROWS), F32))
+        figures[side, c] = lax.fori_loop(0, PER, one, jnp.zeros((8, ROWS), F32), unroll=PER)
 
     def swap(side, c):
         return [
-            remote(give.at[side, seqs(c)], got.at[side, seqs(c)], c_send.at[side, c, 0], c_recv.at[side, c, 0], mate),
-            remote(give_s.at[side, c], got_s.at[side, c], c_send.at[side, c, 1], c_recv.at[side, c, 1], mate),
+            remote(give.at[side, seqs(c)], got.at[side, seqs(c)], c_send.at[0], c_recv.at[side, c, 0], mate),
+            remote(give_s.at[side, c], got_s.at[side, c], c_send.at[1], c_recv.at[side, c, 1], mate),
         ]
 
     def merge_cores(side, c):
@@ -189,14 +192,13 @@
             piece = piece_of((x + dx) % NX, (y + dy) % NY)
             rows = pl.ds(pl.multiple_of(piece * PIECE, PIECE), PIECE)
             target = in_plane(dx, dy)
-            copies.append(remote(plane.at[side, seqs(c), rows], land.at[c, n], a_send.at[c, n, 0], a_recv.at[c, n, 0], target))
-            copies.append(remote(plane_s.at[side, c, piece], land_s.at[c, n], a_send.at[c, n, 1], a_recv.at[c, n, 1], target))
+            copies.append(remote(plane.at[side, seqs(c), rows], land.at[c, n], a_send.at[0], a_recv.at[c, 0], target))
+            copies.append(remote(plane_s.at[side, c, piece], land_s.at[c, n], a_send.at[1], a_recv.at[c, 1], target))
         return copies
 
     def merge_plane(c):
-        for side in range(2):
-            for copy in scatter(side, c):
-                copy.wait_recv()
+        remote(land.at[c], land.at[c], a_send.at[0], a_recv.at[c, 0], mate).wait_recv()
+        remote(land_s.at[c], land_s.at[c], a_send.at[1], a_recv.at[c, 1], mate).wait_recv()
         figures = jnp.concatenate([plane_s[0, c, mine]] + [land_s[c, n] for n in range(len(PLANE))], axis=0)
         peak = jnp.max(figures, axis=0, keepdims=True)
         is_peak = iota((1, ROWS), 1) < SPAN
@@ -213,8 +215,8 @@
         copies = []
         for dz in range(1, NZ):
             target = along_z(dz)
-            copies.append(remote(zed.at[c, (z + dz) % NZ], zland.at[c, dz - 1], z_send.at[c, dz, 0], z_recv.at[c, dz, 0], target))
-            copies.append(remote(zed_s.at[c], zland_s.at[c, dz - 1], z_send.at[c, dz, 1], z_recv.at[c, dz, 1], target))
+            copies.append(remote(zed.at[c, (z + dz) % NZ], zland.at[c, dz - 1], z_send.at[0], z_recv.at[c, 0], target))
+            copies.append(remote(zed_s.at[c], zland_s.at[c, dz - 1], z_send.at[1], z_recv.at[c, 1], target))
         return copies
 
     def draft(c):
@@ -230,8 +232,8 @@
         return tuple(jnp.where(low, a[:SLICE], a[SLICE:]) for a in (peak, total, sums))
 
     def finish(c, drafted):
-        for copy in spread(c):
-            copy.wait_recv()
+        remote(zland.at[c], zland.at[c], z_send.at[0], z_recv.at[c, 0], mate).wait_recv()
+        remote(zland_s.at[c], zland_s.at[c], z_send.at[1], z_recv.at[c, 1], mate).wait_recv()
         figures = jnp.concatenate([zed_s[c]] + [zland_s[c, n] for n in range(NZ - 1)], axis=0)
         peak = jnp.max(figures, axis=0, keepdims=True)
         is_peak = iota((1, ROWS), 1) < SPAN
@@ -250,29 +252,25 @@
 
     def regather(c):
         return [
-            remote(done.at[c, z], done.at[c, z], g_send.at[c, dz], g_recv.at[c, dz], along_z(dz)) for dz in range(1, NZ)
+            remote(done.at[c, z], done.at[c, z], g_send.at[0], g_recv.at[c], along_z(dz)) for dz in range(1, NZ)
         ]
 
     def regathered(c):
-        for dz in range(1, NZ):
-            source = (z + NZ - dz) % NZ
-            remote(done.at[c, z], done.at[c, source], g_send.at[c, dz], g_recv.at[c, dz], along_z(dz)).wait_recv()
+        remote(zland.at[c], zland.at[c], g_send.at[0], g_recv.at[c], mate).wait_recv()
 
     def deliver(c):
         rows = pl.ds(pl.multiple_of(mine * PIECE, PIECE), PIECE)
         part = out_ref.at[seqs(c), rows]
         return [
-            remote(part, part, o_send.at[c, n], o_recv.at[c, n], in_plane(dx, dy)) for n, (dx, dy) in enumerate(NEAR)
+            remote(part, part, o_send.at[0], o_recv.at[c], in_plane(dx, dy)) for dx, dy in NEAR
         ]
 
     def delivered(c):
-        rows = pl.ds(pl.multiple_of(mine * PIECE, PIECE), PIECE)
-        for n, (dx, dy) in enumerate(NEAR):
-            source = piece_of((x + NX - dx) % NX, (y + NY - dy) % NY)
-            there = pl.ds(pl.multiple_of(source * PIECE, PIECE), PIECE)
-            remote(
-                out_ref.at[seqs(c), rows], out_ref.at[seqs(c), there], o_send.at[c, n], o_recv.at[c, n], in_plane(dx, dy)
-            ).wait_recv()
+        part = out_ref.at[seqs(c), pl.ds(0, PIECE * len(NEAR))]
+        remote(part, part, o_send.at[0], o_recv.at[c], mate).wait_recv()
+
+    def all_sent(ref, sem):
+        remote(ref, ref, sem, sem, mate).wait_send()
 
     def start(copies):
         for copy in copies:
@@ -305,8 +303,7 @@
         return carry
 
     def far_own(c):
-        for side in range(2):
-            ask_far(c, side).wait_recv()
+        await_far(c)
         pass_on(c).start()
         attend(2, c, own, own_s, 1)
 
@@ -335,6 +332,11 @@
     lax.fori_loop(0, CHUNKS, far, 0)
     lax.fori_loop(0, CHUNKS, far2, 0)
 
+    all_sent(Q.at[0], q_send.at[0])
+    all_sent(Q.at[0], q_send.at[1])
+    all_sent(Q.at[0], q_send.at[2])
+    all_sent(give, c_send.at[0])
+    all_sent(give_s, c_send.at[1])
     for copy in small[1:]:
         copy.wait()
     drafted = [draft(c) for c in range(CHUNKS)]
@@ -345,18 +347,20 @@
     for c in range(CHUNKS):
         finish(c, drafted[c])
         start(regather(c))
+    all_sent(land, a_send.at[0])
+    all_sent(land_s, a_send.at[1])
+    all_sent(zland, z_send.at[0])
+    all_sent(zland_s, z_send.at[1])
     for c in range(CHUNKS):
         regathered(c)
         rows = pl.ds(pl.multiple_of(mine * PIECE, PIECE), PIECE)
         out_ref[seqs(c), rows] = done[c].reshape(PER, PIECE, WIDTH).astype(BF16)
         start(deliver(c))
 
-    for c in range(CHUNKS):
-        sent = [ask_mate(c), ask_far(c, 0), ask_far(c, 1), pass_on(c)]
-        sent += swap(0, c) + swap(1, c) + scatter(0, c) + scatter(1, c) + spread(c) + regather(c) + deliver(c)
-        for copy in sent:
-            copy.wait_send()
+    all_sent(zland, g_send.at[0])
+    for c in range(CHUNKS):
         delivered(c)
+    all_sent(out_ref.at[:, pl.ds(0, PIECE * len(NEAR))], o_send.at[0])
 
 
 def local(queries, cache_keys, cache_values, draft_keys, draft_values, tree_mask, valid_length):
@@ -387,18 +391,18 @@
         pltpu.VMEM((CHUNKS, NZ, SLICE, WIDTH), F32),
         dma((CHUNKS, 3)),
         dma((4,)),
-        dma((CHUNKS, 4)),
-        dma((CHUNKS, 4)),
+        dma((3,)),
+        dma((3, CHUNKS)),
+        dma((2,)),
         dma((2, CHUNKS, 2)),
-        dma((2, CHUNKS, 2)),
-        dma((CHUNKS, n, 2)),
-        dma((CHUNKS, n, 2)),
-        dma((CHUNKS, NZ, 2)),
-        dma((CHUNKS, NZ, 2)),
-        dma((CHUNKS, NZ)),
-        dma((CHUNKS, NZ)),
-        dma((CHUNKS, len(NEAR))),
-        dma((CHUNKS, len(NEAR))),
+        dma((2,)),
+        dma((CHUNKS, 2)),
+        dma((2,)),
+        dma((CHUNKS, 2)),
+        dma((1,)),
+        dma((CHUNKS,)),
+        dma((1,)),
+        dma((CHUNKS,)),
     ]
     out = pl.pallas_call(
         kernel,
@@ -406,7 +410,7 @@
         in_specs=[pl.BlockSpec(memory_space=pltpu.HBM)] * 7,
         out_specs=pl.BlockSpec(memory_space=pltpu.VMEM),
         scratch_shapes=scratch,
-        compiler_params=pltpu.CompilerParams(collective_id=0, has_side_effects=True, vmem_limit_bytes=48 << 20),
+        compiler_params=pltpu.CompilerParams(collective_id=0, has_side_effects=True, vmem_limit_bytes=60 << 20),
         name="attend",
     )(
         queries.reshape(SEQS, ROWS, WIDTH),

time: 68.2 us -> 46.4 us (0.68)
  Pallas kernels: 59.4 us -> 44.1 us
  local copies, waits for them, and re-layouts: 7.92 us -> 1.77 us
    pallas_call x1, Pallas kernels: 59.4 us -> 44.1 us  [local(): pl.pallas_call(kernel, out_shape=jax.ShapeDtypeStruct((SEQS, ROWS, WIDTH)...]
    unnamed x15 -> x1, local copies, waits for them, and re-layouts: 7.92 us -> 1.77 us
where the time goes in v2:
time: 46.4 us; the launch traced here: 45.9 us
  Pallas kernels  44.1 us (95%)
  local copies, waits for them, and re-layouts  1.77 us (4%)
    pallas_call x1, Pallas kernels, local(): pl.pallas_call(kernel, out_shape=jax.ShapeDtypeStruct((SEQS, ROWS, WIDTH)...  44.1 us
    unnamed x1, local copies, waits for them, and re-layouts  1.77 us

profile of v2, /device:TPU:32, one launch (start us, length us, event | category | flops | bytes accessed | tf_op | source)
XLA Modules:
  0.0 45.9 jit_solution(8239332754248787376)
XLA Ops:
  0.0 44.1 %attend.1 = bf16[12,128,128]{2,1,0:T(8,128)(2,1)} custom-call(bf16[12,128,128]{2,1,0:T(8,128)(2,1)} %bitcast.9, bf16[12,512,128]{2,1,0:T(8,128)(2,1)} %bitcast.6, bf16[12,512,128]{2,1,0:T(8,128)(2,1)} %bitcast.7, bf16[12,32,128]{2,1,0:T(8,128)(2,1)} %bitcast.10, bf16[12,32,128]{2,1,0:T(8,128)(2,1)} %bitcast.11, s32[12,32,32]{2,1,0:T(8,128)} %tm_hbm.1, s32[12]{0:T(128)} %vl_hbm.1), custom_call_target="tpu_custom_call" | custom-call | tf_op jit(solution)/shard_map/attend/pallas_call | solution.py:407
  44.1 1.8 %copy.9 = bf16[1,12,4,32,128]{4,3,2,1,0:T(8,128)(2,1)} copy(bf16[1,12,4,32,128]{4,3,2,1,0:T(8,128)(2,1)} %bitcast.8) | data formatting | bytes 786432

commit v3 on v2

v3 whole, which is shorter than its diff:
```python
import math

import jax
import jax.numpy as jnp
from jax import lax
from jax.experimental import pallas as pl
from jax.experimental.pallas import tpu as pltpu
from jax.sharding import PartitionSpec as P

MESH = pl.DeviceIdType.MESH
F32 = jnp.float32
BF16 = jnp.bfloat16

SEQS = 12
ROWS = 128
KEYS = 512
WIDTH = 128
DRAFT = 32
NX, NY, NZ = 4, 4, 8
CHUNKS = 3
PER = SEQS // CHUNKS
PIECE = 16
SPAN = PER * PIECE
NEAR = [(dx, dy) for dy in (0, 2) for dx in range(NX) if (dx, dy) != (0, 0)]
FAR = [(dx, dy) for dx in range(NX) for dy in (1, 3)]

SCALE = math.log2(math.e) / math.sqrt(WIDTH)
FLOOR = -1e30
LOW = -1e29


def iota(shape, axis):
    return lax.broadcasted_iota(jnp.int32, shape, axis)


def to_row(column):
    eye = iota((ROWS, ROWS), 0) == iota((ROWS, ROWS), 1)
    return jnp.sum(jnp.where(eye, column, 0.0), axis=0, keepdims=True)


def to_column(row, rows, first):
    pick = iota((rows, ROWS), 1) == iota((rows, ROWS), 0) + first
    return jnp.sum(jnp.where(pick, row, 0.0), axis=1, keepdims=True)


def by_piece(tile):
    lane = iota((8, ROWS), 1) // PIECE
    sub = iota((8, ROWS), 0)
    out = jnp.zeros((8, ROWS), F32)
    for d in range(8):
        moved = tile if d == 0 else pltpu.roll(tile, PIECE * d, 1)
        diagonal = jnp.sum(jnp.where(lane == sub, moved, 0.0), axis=0, keepdims=True)
        out = jnp.where((lane - sub + 8) % 8 == d, diagonal, out)
    return out


def kernel(
    q_hbm, k_hbm, v_hbm, dk_hbm, dv_hbm, tm_hbm, vl_hbm, out_ref,
    Q, K, V, DK, DV, TM, VL,
    plane, plane_s, xland, xland_s, half_sum, half_s, land, land_s,
    zed, zed_s, zland, zland_s, drafted, drafted_s,
    ld, ld_small, q_send, q_recv, c_send, c_recv, n_send, n_recv, a_send, a_recv, z_send, z_recv, g_send, g_recv, o_send, o_recv,
):
    loop_index = lax.axis_index("loop")
    group_index = lax.axis_index("grp")
    core = loop_index % 2
    x = group_index % NX
    z = (group_index // NX) % NZ
    y = (group_index // (NX * NZ)) * 2 + loop_index // 2

    def device(px, py, pz, pc):
        return ((py % 2) * 2 + pc, ((py // 2) * NZ + pz) * NX + px)

    mate = device(x, y, z, 1 - core)

    def in_plane(dx, dy):
        return device((x + dx) % NX, (y + dy) % NY, z, core)

    def piece_of(px, py):
        return px * 2 + py // 2

    mine = piece_of(x, y)

    def remote(src, dst, send, recv, target):
        return pltpu.make_async_remote_copy(
            src_ref=src, dst_ref=dst, send_sem=send, recv_sem=recv, device_id=target, device_id_type=MESH
        )

    lead = z == 0
    peers = [mate, in_plane(0, 1), in_plane(0, 3)]
    peers += [in_plane(dx, dy) for dx, dy in FAR + NEAR if (dx, dy % 2) != (0, 1)]
    others = [device(x, y, other, core) for other in (1, 7, 2, 6, 3, 5, 4)]
    leader = device(x, y, 0, core)
    barrier = pltpu.get_barrier_semaphore()

    def greet(targets):
        for target in targets:
            pl.semaphore_signal(barrier, inc=1, device_id=target, device_id_type=MESH)

    greet(peers)
    pl.when(lead)(lambda: greet(others))
    pl.when(jnp.logical_not(lead))(lambda: greet([leader]))

    def seqs(c):
        return pl.ds(c * PER, PER)

    def load(c):
        return [
            pltpu.make_async_copy(q_hbm.at[seqs(c)], Q.at[0, seqs(c)], ld.at[c, 0]),
            pltpu.make_async_copy(k_hbm.at[seqs(c)], K.at[seqs(c), 0], ld.at[c, 1]),
            pltpu.make_async_copy(v_hbm.at[seqs(c)], V.at[seqs(c), 0], ld.at[c, 2]),
        ]

    small = [
        pltpu.make_async_copy(vl_hbm, VL, ld_small.at[0]),
        pltpu.make_async_copy(dk_hbm, DK, ld_small.at[1]),
        pltpu.make_async_copy(dv_hbm, DV, ld_small.at[2]),
        pltpu.make_async_copy(tm_hbm, TM, ld_small.at[3]),
    ]
    small[0].start()
    for c in range(CHUNKS):
        for copy in load(c):
            copy.start()
    for copy in small[1:]:
        copy.start()

    half = ROWS // 2

    def to_mate(c):
        return [
            remote(k_hbm.at[seqs(c)], K.at[seqs(c), 1], c_send.at[0], c_recv.at[c, 0], mate),
            remote(v_hbm.at[seqs(c)], V.at[seqs(c), 1], c_send.at[1], c_recv.at[c, 1], mate),
        ]

    def ask_far(c, side):
        rows = pl.ds(side * half, half)
        return remote(
            q_hbm.at[seqs(c), rows], Q.at[1, seqs(c), rows], q_send.at[0], q_recv.at[c],
            in_plane(0, 1 if side == 0 else 3),
        )

    def await_far(c):
        remote(Q.at[1, seqs(c)], Q.at[1, seqs(c)], q_send.at[0], q_recv.at[c], mate).wait_recv()

    def first(member):
        return (member * (NX * 2 * NZ) + group_index) * KEYS

    lane = iota((1, 2 * KEYS), 1)
    position = jnp.where(lane < KEYS, first(loop_index), first(loop_index + 1 - 2 * core) - KEYS) + lane
    ones = jnp.ones((2 * KEYS, WIDTH), BF16)
    sub8 = iota((8, ROWS), 0)

    def attend(side, c):
        def one(i, tile):
            s = c * PER + i
            scores = lax.dot_general(Q[side, s], K[s].reshape(2 * KEYS, WIDTH), (((1,), (1,)), ((), ())), preferred_element_type=F32)
            scores = jnp.where(position < VL[s], scores * SCALE, FLOOR)
            peak = jnp.maximum(jnp.max(scores, axis=1, keepdims=True), LOW)
            weights = jnp.exp2(scores - peak).astype(BF16)
            values = jnp.concatenate([V[s].reshape(2 * KEYS, WIDTH), ones], axis=1)
            both = jnp.dot(weights, values, preferred_element_type=F32)
            plane[side, s] = both[:, :WIDTH].astype(BF16)
            tile = jnp.where(sub8 == i, to_row(peak), tile)
            return jnp.where(sub8 == PER + i, to_row(both[:, WIDTH:]), tile)

        pieces = by_piece(lax.fori_loop(0, PER, one, jnp.zeros((8, ROWS), F32), unroll=PER))
        for p in range(8):
            plane_s[side, c, p] = pieces[p : p + 1]

    def piece_rows(piece, count=1):
        return pl.ds(pl.multiple_of(piece * PIECE, PIECE), count * PIECE)

    def scatter_x(c):
        copies = []
        for dx in range(1, NX):
            pair = ((x + dx) % NX) * 2
            target = in_plane(dx, 0)
            copies.append(
                remote(plane.at[0, seqs(c), piece_rows(pair, 2)], xland.at[c, dx - 1], n_send.at[0], n_recv.at[c, 0], target)
            )
            copies.append(
                remote(plane_s.at[0, c, pl.ds(pair, 2)], xland_s.at[c, dx - 1], n_send.at[1], n_recv.at[c, 1], target)
            )
        return copies

    def scatter_far(c):
        copies = []
        for n, (dx, dy) in enumerate(FAR):
            piece = piece_of((x + dx) % NX, (y + dy) % NY)
            target = in_plane(dx, dy)
            copies.append(remote(plane.at[1, seqs(c), piece_rows(piece)], land.at[c, n], a_send.at[0], a_recv.at[c, 0], target))
            copies.append(remote(plane_s.at[1, c, piece], land_s.at[c, n], a_send.at[1], a_recv.at[c, 1], target))
        return copies

    def across(c):
        n, target = len(FAR), in_plane(0, 2)
        return [
            remote(half_sum.at[c], land.at[c, n], a_send.at[0], a_recv.at[c, 0], target),
            remote(half_s.at[c], land_s.at[c, n], a_send.at[1], a_recv.at[c, 1], target),
        ]

    def merge(figures, parts):
        peak = jnp.max(figures, axis=0, keepdims=True)
        is_peak = iota((1, ROWS), 1) < SPAN
        factor = jnp.exp2(jnp.where(is_peak, figures - peak, 0.0))
        total = jnp.sum(pltpu.roll(factor, SPAN, 1) * figures, axis=0, keepdims=True)
        acc = jnp.zeros((SPAN, WIDTH), F32)
        for n, part in enumerate(parts):
            acc += part.reshape(SPAN, WIDTH).astype(F32) * to_column(factor[n : n + 1], SPAN, 0)
        return jnp.where(is_peak, peak, total), acc

    def near_sources(c, level):
        piece = x * 2 + level
        rows = pl.ds(pl.multiple_of(level * PIECE, PIECE), PIECE)
        figures = [plane_s[0, c, piece]] + [xland_s[c, n, level] for n in range(NX - 1)]
        parts = [plane[0, seqs(c), piece_rows(piece)]] + [xland[c, n, :, rows] for n in range(NX - 1)]
        return figures, parts

    def merge_across(c):
        remote(xland.at[c], xland.at[c], n_send.at[0], n_recv.at[c, 0], mate).wait_recv()
        remote(xland_s.at[c], xland_s.at[c], n_send.at[1], n_recv.at[c, 1], mate).wait_recv()
        figures, parts = near_sources(c, 1 - y // 2)
        row, acc = merge(jnp.concatenate(figures, axis=0), parts)
        half_s[c] = row
        half_sum[c] = acc.reshape(PER, PIECE, WIDTH).astype(BF16)
        start(across(c))

    def merge_plane(c):
        remote(land.at[c], land.at[c], a_send.at[0], a_recv.at[c, 0], mate).wait_recv()
        remote(land_s.at[c], land_s.at[c], a_send.at[1], a_recv.at[c, 1], mate).wait_recv()
        figures, parts = near_sources(c, y // 2)
        figures += [land_s[c, n] for n in range(len(FAR) + 1)]
        parts += [land[c, n] for n in range(len(FAR) + 1)]
        row, acc = merge(jnp.concatenate(figures, axis=0), parts)
        zed_s[c] = row
        zed[c] = acc.reshape(PER, PIECE, WIDTH).astype(BF16)

    def to_leader(c):
        return [
            remote(zed.at[c], zland.at[c, z - 1], z_send.at[0], z_recv.at[c, 0], leader),
            remote(zed_s.at[c], zland_s.at[c, z - 1], z_send.at[1], z_recv.at[c, 1], leader),
        ]

    def draft(c):
        allowed_rows = pl.ds(pl.multiple_of((mine % 2) * PIECE, PIECE), PIECE)
        for i in range(PER):
            s = c * PER + i
            queries = Q[0, s, piece_rows(mine)]
            scores = lax.dot_general(queries, DK[s], (((1,), (1,)), ((), ())), preferred_element_type=F32) * SCALE
            allowed = TM[s, allowed_rows] == 1
            peak = jnp.max(jnp.where(allowed, scores, FLOOR), axis=1, keepdims=True)
            weights = jnp.where(allowed, jnp.exp2(scores - peak), 0.0).astype(BF16)
            total = jnp.sum(weights.astype(F32), axis=1, keepdims=True)
            rows = pl.ds(i * PIECE, PIECE)
            drafted[c, rows] = jnp.dot(weights, DV[s], preferred_element_type=F32)
            drafted_s[c, 0, rows] = jnp.broadcast_to(peak, (PIECE, WIDTH))
            drafted_s[c, 1, rows] = jnp.broadcast_to(total, (PIECE, WIDTH))

    def finish(c):
        remote(zland.at[c], zland.at[c], z_send.at[0], z_recv.at[c, 0], mate).wait_recv()
        remote(zland_s.at[c], zland_s.at[c], z_send.at[1], z_recv.at[c, 1], mate).wait_recv()
        figures = jnp.concatenate([zed_s[c]] + [zland_s[c, n] for n in range(NZ - 1)], axis=0)
        row, acc = merge(figures, [zed[c]] + [zland[c, n] for n in range(NZ - 1)])
        top, total = to_column(row, SPAN, 0), to_column(row, SPAN, SPAN)
        joined = jnp.maximum(top, drafted_s[c, 0])
        fa, fb = jnp.exp2(top - joined), jnp.exp2(drafted_s[c, 0] - joined)
        result = (acc * fa + drafted[c] * fb) / (total * fa + drafted_s[c, 1] * fb)
        out_ref[seqs(c), piece_rows(mine)] = result.reshape(PER, PIECE, WIDTH).astype(BF16)

    def from_leader(c, targets):
        part = out_ref.at[seqs(c), piece_rows(mine)]
        return [remote(part, part, g_send.at[0], g_recv.at[c], target) for target in targets]

    def deliver(c):
        rows = pl.ds(pl.multiple_of(mine * PIECE, PIECE), PIECE)
        part = out_ref.at[seqs(c), rows]
        return [
            remote(part, part, o_send.at[0], o_recv.at[c], in_plane(dx, dy)) for dx, dy in NEAR
        ]

    def delivered(c):
        part = out_ref.at[seqs(c), pl.ds(0, PIECE * len(NEAR))]
        remote(part, part, o_send.at[0], o_recv.at[c], mate).wait_recv()

    def all_sent(ref, sem):
        remote(ref, ref, sem, sem, mate).wait_send()

    def start(copies):
        for copy in copies:
            copy.start()

    pl.semaphore_wait(barrier, len(peers) + jnp.where(lead, NZ - 1, 1))
    for c in range(CHUNKS):
        for side in range(2):
            ask_far(c, side).start()
    for c in range(CHUNKS):
        start(to_mate(c))

    small[0].wait()

    def near(c, carry):
        for copy in load(c):
            copy.wait()
        for copy in to_mate(c):
            copy.wait_recv()
        attend(0, c)
        start(scatter_x(c))
        return carry

    def far(c):
        await_far(c)
        attend(1, c)
        start(scatter_far(c))

    lax.fori_loop(0, CHUNKS, near, 0)

    def step(i, carry):
        pl.when(i < CHUNKS)(lambda: far(i))
        pl.when(i >= 1)(lambda: merge_across(i - 1))
        return carry

    lax.fori_loop(0, CHUNKS + 1, step, 0)

    all_sent(Q.at[0], q_send.at[0])
    all_sent(K.at[:, 0], c_send.at[0])
    all_sent(V.at[:, 0], c_send.at[1])
    for copy in small[1:]:
        copy.wait()

    @pl.when(lead)
    def _():
        for c in range(CHUNKS):
            draft(c)

    for c in range(CHUNKS):
        merge_plane(c)

        @pl.when(jnp.logical_not(lead))
        def _():
            start(to_leader(c))

    all_sent(xland, n_send.at[0])
    all_sent(xland_s, n_send.at[1])
    all_sent(land, a_send.at[0])
    all_sent(land_s, a_send.at[1])

    for c in range(CHUNKS):

        @pl.when(lead)
        def _():
            finish(c)
            start(from_leader(c, others))

        @pl.when(jnp.logical_not(lead))
        def _():
            from_leader(c, [leader])[0].wait_recv()

        start(deliver(c))

    @pl.when(lead)
    def _():
        part = out_ref.at[:, pl.ds(0, PIECE * (NZ - 1))]
        all_sent(part, g_send.at[0])

    @pl.when(jnp.logical_not(lead))
    def _():
        all_sent(zed, z_send.at[0])
        all_sent(zed_s, z_send.at[1])

    for c in range(CHUNKS):
        delivered(c)
    all_sent(out_ref.at[:, pl.ds(0, PIECE * len(NEAR))], o_send.at[0])


def local(queries, cache_keys, cache_values, draft_keys, draft_values, tree_mask, valid_length):
    dma = pltpu.SemaphoreType.DMA
    n = len(FAR) + 1
    scratch = [
        pltpu.VMEM((2, SEQS, ROWS, WIDTH), BF16),
        pltpu.VMEM((SEQS, 2, KEYS, WIDTH), BF16),
        pltpu.VMEM((SEQS, 2, KEYS, WIDTH), BF16),
        pltpu.VMEM((SEQS, DRAFT, WIDTH), BF16),
        pltpu.VMEM((SEQS, DRAFT, WIDTH), BF16),
        pltpu.VMEM((SEQS, DRAFT, DRAFT), jnp.int32),
        pltpu.SMEM((SEQS,), jnp.int32),
        pltpu.VMEM((2, SEQS, ROWS, WIDTH), BF16),
        pltpu.VMEM((2, CHUNKS, 8, 1, ROWS), F32),
        pltpu.VMEM((CHUNKS, NX - 1, PER, 2 * PIECE, WIDTH), BF16),
        pltpu.VMEM((CHUNKS, NX - 1, 2, 1, ROWS), F32),
        pltpu.VMEM((CHUNKS, PER, PIECE, WIDTH), BF16),
        pltpu.VMEM((CHUNKS, 1, ROWS), F32),
        pltpu.VMEM((CHUNKS, n, PER, PIECE, WIDTH), BF16),
        pltpu.VMEM((CHUNKS, n, 1, ROWS), F32),
        pltpu.VMEM((CHUNKS, PER, PIECE, WIDTH), BF16),
        pltpu.VMEM((CHUNKS, 1, ROWS), F32),
        pltpu.VMEM((CHUNKS, NZ - 1, PER, PIECE, WIDTH), BF16),
        pltpu.VMEM((CHUNKS, NZ - 1, 1, ROWS), F32),
        pltpu.VMEM((CHUNKS, SPAN, WIDTH), F32),
        pltpu.VMEM((CHUNKS, 2, SPAN, WIDTH), F32),
        dma((CHUNKS, 3)),
        dma((4,)),
        dma((1,)),
        dma((CHUNKS,)),
        dma((2,)),
        dma((CHUNKS, 2)),
        dma((2,)),
        dma((CHUNKS, 2)),
        dma((2,)),
        dma((CHUNKS, 2)),
        dma((2,)),
        dma((CHUNKS, 2)),
        dma((1,)),
        dma((CHUNKS,)),
        dma((1,)),
        dma((CHUNKS,)),
    ]
    out = pl.pallas_call(
        kernel,
        out_shape=jax.ShapeDtypeStruct((SEQS, ROWS, WIDTH), BF16),
        in_specs=[pl.BlockSpec(memory_space=pltpu.HBM)] * 7,
        out_specs=pl.BlockSpec(memory_space=pltpu.VMEM),
        scratch_shapes=scratch,
        compiler_params=pltpu.CompilerParams(collective_id=0, has_side_effects=True, vmem_limit_bytes=60 << 20),
        name="attend",
    )(
        queries.reshape(SEQS, ROWS, WIDTH),
        cache_keys.reshape(SEQS, KEYS, WIDTH),
        cache_values.reshape(SEQS, KEYS, WIDTH),
        draft_keys.reshape(SEQS, DRAFT, WIDTH),
        draft_values.reshape(SEQS, DRAFT, WIDTH),
        tree_mask,
        valid_length,
    )
    return out.reshape(queries.shape)


def solution(mesh):
    in_specs = (
        P(None, None, "loop", None, None),
        P(None, None, ("loop", "grp"), None),
        P(None, None, ("loop", "grp"), None),
        P(),
        P(),
        P(),
        P(),
    )
    out_specs = P(None, None, "loop", None, None)
    return jax.shard_map(local, mesh=mesh, in_specs=in_specs, out_specs=out_specs, check_vma=False)
```

time: 46.4 us -> 42.3 us (0.912)
  Pallas kernels: 44.1 us -> 40.4 us
    pallas_call x1, Pallas kernels: 44.1 us -> 40.4 us  [local(): pl.pallas_call(kernel, out_shape=jax.ShapeDtypeStruct((SEQS, ROWS, WIDTH)...]
where the time goes in v3:
time: 42.3 us; the launch traced here: 42.2 us
  Pallas kernels  40.4 us (96%)
  local copies, waits for them, and re-layouts  1.77 us (4%)
    pallas_call x1, Pallas kernels, local(): pl.pallas_call(kernel, out_shape=jax.ShapeDtypeStruct((SEQS, ROWS, WIDTH)...  40.4 us
    unnamed x1, local copies, waits for them, and re-layouts  1.77 us

profile of v3, /device:TPU:32, one launch (start us, length us, event | category | flops | bytes accessed | tf_op | source)
XLA Modules:
  0.0 42.2 jit_solution(5823221188978600820)
XLA Ops:
  0.0 40.4 %attend.1 = bf16[12,128,128]{2,1,0:T(8,128)(2,1)} custom-call(bf16[12,128,128]{2,1,0:T(8,128)(2,1)} %bitcast.9, bf16[12,512,128]{2,1,0:T(8,128)(2,1)} %bitcast.6, bf16[12,512,128]{2,1,0:T(8,128)(2,1)} %bitcast.7, bf16[12,32,128]{2,1,0:T(8,128)(2,1)} %bitcast.10, bf16[12,32,128]{2,1,0:T(8,128)(2,1)} %bitcast.11, s32[12,32,32]{2,1,0:T(8,128)} %tm_hbm.1, s32[12]{0:T(128)} %vl_hbm.1), custom_call_target="tpu_custom_call" | custom-call | tf_op jit(solution)/shard_map/attend/pallas_call | solution.py:417
  40.4 1.8 %copy.9 = bf16[1,12,4,32,128]{4,3,2,1,0:T(8,128)(2,1)} copy(bf16[1,12,4,32,128]{4,3,2,1,0:T(8,128)(2,1)} %bitcast.8) | data formatting | bytes 786432

commit v4 on v3

--- a/solution.py
+++ b/solution.py
@@ -58,7 +58,7 @@
     q_hbm, k_hbm, v_hbm, dk_hbm, dv_hbm, tm_hbm, vl_hbm, out_ref,
     Q, K, V, DK, DV, TM, VL,
     plane, plane_s, xland, xland_s, half_sum, half_s, land, land_s,
-    zed, zed_s, zland, zland_s, drafted, drafted_s,
+    zed, zed_s, zland, zland_s, drafted, drafted_s, final,
     ld, ld_small, q_send, q_recv, c_send, c_recv, n_send, n_recv, a_send, a_recv, z_send, z_recv, g_send, g_recv, o_send, o_recv,
 ):
     loop_index = lax.axis_index("loop")
@@ -150,22 +150,29 @@
     ones = jnp.ones((2 * KEYS, WIDTH), BF16)
     sub8 = iota((8, ROWS), 0)
 
-    def attend(side, c):
-        def one(i, tile):
+    def attend(sides, c):
+        def one(i, tiles):
             s = c * PER + i
-            scores = lax.dot_general(Q[side, s], K[s].reshape(2 * KEYS, WIDTH), (((1,), (1,)), ((), ())), preferred_element_type=F32)
-            scores = jnp.where(position < VL[s], scores * SCALE, FLOOR)
-            peak = jnp.maximum(jnp.max(scores, axis=1, keepdims=True), LOW)
-            weights = jnp.exp2(scores - peak).astype(BF16)
             values = jnp.concatenate([V[s].reshape(2 * KEYS, WIDTH), ones], axis=1)
-            both = jnp.dot(weights, values, preferred_element_type=F32)
-            plane[side, s] = both[:, :WIDTH].astype(BF16)
-            tile = jnp.where(sub8 == i, to_row(peak), tile)
-            return jnp.where(sub8 == PER + i, to_row(both[:, WIDTH:]), tile)
-
-        pieces = by_piece(lax.fori_loop(0, PER, one, jnp.zeros((8, ROWS), F32), unroll=PER))
-        for p in range(8):
-            plane_s[side, c, p] = pieces[p : p + 1]
+            out = []
+            for side, tile in zip(sides, tiles):
+                scores = lax.dot_general(
+                    Q[side, s], K[s].reshape(2 * KEYS, WIDTH), (((1,), (1,)), ((), ())), preferred_element_type=F32
+                )
+                scores = jnp.where(position < VL[s], scores * SCALE, FLOOR)
+                peak = jnp.maximum(jnp.max(scores, axis=1, keepdims=True), LOW)
+                weights = jnp.exp2(scores - peak).astype(BF16)
+                both = jnp.dot(weights, values, preferred_element_type=F32)
+                plane[side, s] = both[:, :WIDTH].astype(BF16)
+                tile = jnp.where(sub8 == i, to_row(peak), tile)
+                out.append(jnp.where(sub8 == PER + i, to_row(both[:, WIDTH:]), tile))
+            return tuple(out)
+
+        tiles = lax.fori_loop(0, PER, one, (jnp.zeros((8, ROWS), F32),) * len(sides), unroll=PER)
+        for side, tile in zip(sides, tiles):
+            pieces = by_piece(tile)
+            for p in range(8):
+                plane_s[side, c, p] = pieces[p : p + 1]
 
     def piece_rows(piece, count=1):
         return pl.ds(pl.multiple_of(piece * PIECE, PIECE), count * PIECE)
@@ -265,18 +272,17 @@
         joined = jnp.maximum(top, drafted_s[c, 0])
         fa, fb = jnp.exp2(top - joined), jnp.exp2(drafted_s[c, 0] - joined)
         result = (acc * fa + drafted[c] * fb) / (total * fa + drafted_s[c, 1] * fb)
-        out_ref[seqs(c), piece_rows(mine)] = result.reshape(PER, PIECE, WIDTH).astype(BF16)
+        final[c] = result.reshape(PER, PIECE, WIDTH).astype(BF16)
 
     def from_leader(c, targets):
-        part = out_ref.at[seqs(c), piece_rows(mine)]
-        return [remote(part, part, g_send.at[0], g_recv.at[c], target) for target in targets]
+        return [remote(final.at[c], final.at[c], g_send.at[0], g_recv.at[c], target) for target in targets]
+
+    def keep(c):
+        return pltpu.make_async_copy(final.at[c], out_ref.at[seqs(c), piece_rows(mine)], ld.at[c, 0])
 
     def deliver(c):
-        rows = pl.ds(pl.multiple_of(mine * PIECE, PIECE), PIECE)
-        part = out_ref.at[seqs(c), rows]
-        return [
-            remote(part, part, o_send.at[0], o_recv.at[c], in_plane(dx, dy)) for dx, dy in NEAR
-        ]
+        place = out_ref.at[seqs(c), piece_rows(mine)]
+        return [remote(final.at[c], place, o_send.at[0], o_recv.at[c], in_plane(dx, dy)) for dx, dy in NEAR]
 
     def delivered(c):
         part = out_ref.at[seqs(c), pl.ds(0, PIECE * len(NEAR))]
@@ -298,28 +304,27 @@
 
     small[0].wait()
 
-    def near(c, carry):
+    def near(c):
         for copy in load(c):
             copy.wait()
         for copy in to_mate(c):
             copy.wait_recv()
-        attend(0, c)
+        attend((0,), c)
         start(scatter_x(c))
-        return carry
 
     def far(c):
         await_far(c)
-        attend(1, c)
+        attend((1,), c)
         start(scatter_far(c))
 
-    lax.fori_loop(0, CHUNKS, near, 0)
-
-    def step(i, carry):
-        pl.when(i < CHUNKS)(lambda: far(i))
-        pl.when(i >= 1)(lambda: merge_across(i - 1))
-        return carry
-
-    lax.fori_loop(0, CHUNKS + 1, step, 0)
+    for c in range(CHUNKS):
+        near(c)
+    far(0)
+    far(1)
+    merge_across(0)
+    far(2)
+    merge_across(1)
+    merge_across(2)
 
     all_sent(Q.at[0], q_send.at[0])
     all_sent(K.at[:, 0], c_send.at[0])
@@ -355,12 +360,11 @@
         def _():
             from_leader(c, [leader])[0].wait_recv()
 
-        start(deliver(c))
+        start(deliver(c) + [keep(c)])
 
     @pl.when(lead)
     def _():
-        part = out_ref.at[:, pl.ds(0, PIECE * (NZ - 1))]
-        all_sent(part, g_send.at[0])
+        all_sent(zland, g_send.at[0])
 
     @pl.when(jnp.logical_not(lead))
     def _():
@@ -369,7 +373,8 @@
 
     for c in range(CHUNKS):
         delivered(c)
-    all_sent(out_ref.at[:, pl.ds(0, PIECE * len(NEAR))], o_send.at[0])
+        keep(c).wait()
+    all_sent(zland, o_send.at[0])
 
 
 def local(queries, cache_keys, cache_values, draft_keys, draft_values, tree_mask, valid_length):
@@ -397,6 +402,7 @@
         pltpu.VMEM((CHUNKS, NZ - 1, 1, ROWS), F32),
         pltpu.VMEM((CHUNKS, SPAN, WIDTH), F32),
         pltpu.VMEM((CHUNKS, 2, SPAN, WIDTH), F32),
+        pltpu.VMEM((CHUNKS, PER, PIECE, WIDTH), BF16),
         dma((CHUNKS, 3)),
         dma((4,)),
         dma((1,)),
@@ -414,15 +420,7 @@
         dma((1,)),
         dma((CHUNKS,)),
     ]
-    out = pl.pallas_call(
-        kernel,
-        out_shape=jax.ShapeDtypeStruct((SEQS, ROWS, WIDTH), BF16),
-        in_specs=[pl.BlockSpec(memory_space=pltpu.HBM)] * 7,
-        out_specs=pl.BlockSpec(memory_space=pltpu.VMEM),
-        scratch_shapes=scratch,
-        compiler_params=pltpu.CompilerParams(collective_id=0, has_side_effects=True, vmem_limit_bytes=60 << 20),
-        name="attend",
-    )(
+    operands = [
         queries.reshape(SEQS, ROWS, WIDTH),
         cache_keys.reshape(SEQS, KEYS, WIDTH),
         cache_values.reshape(SEQS, KEYS, WIDTH),
@@ -430,6 +428,18 @@
         draft_values.reshape(SEQS, DRAFT, WIDTH),
         tree_mask,
         valid_length,
+    ]
+    operands = [pltpu.with_memory_space_constraint(a, pltpu.HBM) for a in operands]
+    out = pl.pallas_call(
+        kernel,
+        out_shape=pltpu.VMEM((SEQS, ROWS, WIDTH), BF16),
+        in_specs=[pl.BlockSpec(memory_space=pltpu.HBM)] * 7,
+        out_specs=pl.BlockSpec(memory_space=pltpu.VMEM),
+        scratch_shapes=scratch,
+        compiler_params=pltpu.CompilerParams(collective_id=0, has_side_effects=True, vmem_limit_bytes=40 << 20),
+        name="attend",
+    )(
+        *operands,
     )
     return out.reshape(queries.shape)
 

time: 42.3 us -> 40.5 us (0.957)
  local copies, waits for them, and re-layouts: 1.77 us -> 0.75 us
  Pallas kernels: 40.4 us -> 39.7 us
    unnamed x1, local copies, waits for them, and re-layouts: 1.77 us -> 0.75 us
    pallas_call x1, Pallas kernels: 40.4 us -> 39.7 us  [local(): pl.pallas_call(kernel, out_shape=pltpu.VMEM((SEQS, ROWS, WIDTH), BF16), i...]
where the time goes in v4:
time: 40.5 us
  Pallas kernels  39.7 us (98%)
  local copies, waits for them, and re-layouts  0.75 us (2%)
    pallas_call x1, Pallas kernels, local(): pl.pallas_call(kernel, out_shape=pltpu.VMEM((SEQS, ROWS, WIDTH), BF16), i...  39.7 us

profile of v4, /device:TPU:32, one launch (start us, length us, event | category | flops | bytes accessed | tf_op | source)
XLA Modules:
  0.0 40.5 jit_solution(4808149335412277869)
XLA Ops:
  0.0 39.7 %attend.1 = bf16[12,128,128]{2,1,0:T(8,128)(2,1)S(1)} custom-call(bf16[12,128,128]{2,1,0:T(8,128)(2,1)} %bitcast.9, bf16[12,512,128]{2,1,0:T(8,128)(2,1)} %bitcast.7, bf16[12,512,128]{2,1,0:T(8,128)(2,1)} %bitcast.8, bf16[12,32,128]{2,1,0:T(8,128)(2,1)} %bitcast.10, bf16[12,32,128]{2,1,0:T(8,128)(2,1)} %bitcast.11, s32[12,32,32]{2,1,0:T(8,128)} %tm_hbm.1, ...), custom_call_target="tpu_custom_call" | custom-call | tf_op jit(solution)/shard_map/attend/pallas_call | solution.py:433
  39.7 0.7 %copy.9 = bf16[1,12,4,32,128]{4,3,2,1,0:T(8,128)(2,1)} copy(bf16[1,12,4,32,128]{4,3,2,1,0:T(8,128)(2,1)S(1)} %bitcast.6) | data formatting | bytes 786432

commit v5 on v4

--- a/solution.py
+++ b/solution.py
@@ -319,12 +319,9 @@
 
     for c in range(CHUNKS):
         near(c)
-    far(0)
-    far(1)
-    merge_across(0)
-    far(2)
-    merge_across(1)
-    merge_across(2)
+    for c in range(CHUNKS):
+        far(c)
+        merge_across(c)
 
     all_sent(Q.at[0], q_send.at[0])
     all_sent(K.at[:, 0], c_send.at[0])

time: 40.5 us -> 39.5 us (0.975)
  Pallas kernels: 39.7 us -> 38.6 us
    pallas_call x1, Pallas kernels: 39.7 us -> 38.6 us  [local(): pl.pallas_call(kernel, out_shape=pltpu.VMEM((SEQS, ROWS, WIDTH), BF16), i...]
where the time goes in v5:
time: 39.5 us; the launch traced here: 39.4 us
  Pallas kernels  38.6 us (98%)
  local copies, waits for them, and re-layouts  0.75 us (2%)
    pallas_call x1, Pallas kernels, local(): pl.pallas_call(kernel, out_shape=pltpu.VMEM((SEQS, ROWS, WIDTH), BF16), i...  38.6 us

profile of v5, /device:TPU:32, one launch (start us, length us, event | category | flops | bytes accessed | tf_op | source)
XLA Modules:
  0.0 39.4 jit_solution(6583858406549823671)
XLA Ops:
  0.0 38.6 %attend.1 = bf16[12,128,128]{2,1,0:T(8,128)(2,1)S(1)} custom-call(bf16[12,128,128]{2,1,0:T(8,128)(2,1)} %bitcast.9, bf16[12,512,128]{2,1,0:T(8,128)(2,1)} %bitcast.7, bf16[12,512,128]{2,1,0:T(8,128)(2,1)} %bitcast.8, bf16[12,32,128]{2,1,0:T(8,128)(2,1)} %bitcast.10, bf16[12,32,128]{2,1,0:T(8,128)(2,1)} %bitcast.11, s32[12,32,32]{2,1,0:T(8,128)} %tm_hbm.1, ...), custom_call_target="tpu_custom_call" | custom-call | tf_op jit(solution)/shard_map/attend/pallas_call | solution.py:430
  38.7 0.7 %copy.9 = bf16[1,12,4,32,128]{4,3,2,1,0:T(8,128)(2,1)} copy(bf16[1,12,4,32,128]{4,3,2,1,0:T(8,128)(2,1)S(1)} %bitcast.6) | data formatting | bytes 786432

commit v6 on v5

--- a/solution.py
+++ b/solution.py
@@ -21,8 +21,8 @@
 PER = SEQS // CHUNKS
 PIECE = 16
 SPAN = PER * PIECE
-NEAR = [(dx, dy) for dy in (0, 2) for dx in range(NX) if (dx, dy) != (0, 0)]
-FAR = [(dx, dy) for dx in range(NX) for dy in (1, 3)]
+NEAR = [(dx, dy) for dy in (2, 0) for dx in (2, 1, 3, 0) if (dx, dy) != (0, 0)]
+FAR = [(dx, dy) for dx in (2, 1, 3, 0) for dy in (1, 3)]
 
 SCALE = math.log2(math.e) / math.sqrt(WIDTH)
 FLOOR = -1e30
@@ -89,7 +89,7 @@
     lead = z == 0
     peers = [mate, in_plane(0, 1), in_plane(0, 3)]
     peers += [in_plane(dx, dy) for dx, dy in FAR + NEAR if (dx, dy % 2) != (0, 1)]
-    others = [device(x, y, other, core) for other in (1, 7, 2, 6, 3, 5, 4)]
+    others = [device(x, y, other, core) for other in (1, 2, 3, 4, 7, 6, 5)]
     leader = device(x, y, 0, core)
     barrier = pltpu.get_barrier_semaphore()
 
@@ -179,7 +179,7 @@
 
     def scatter_x(c):
         copies = []
-        for dx in range(1, NX):
+        for dx in (2, 1, 3):
             pair = ((x + dx) % NX) * 2
             target = in_plane(dx, 0)
             copies.append(

time: 39.5 us -> 39 us (0.987)
  Pallas kernels: 38.6 us -> 38.2 us
    pallas_call x1, Pallas kernels: 38.6 us -> 38.2 us  [local(): pl.pallas_call(kernel, out_shape=pltpu.VMEM((SEQS, ROWS, WIDTH), BF16), i...]
where the time goes in v6:
time: 39 us; the launch traced here: 38.9 us
  Pallas kernels  38.2 us (98%)
  local copies, waits for them, and re-layouts  0.75 us (2%)
    pallas_call x1, Pallas kernels, local(): pl.pallas_call(kernel, out_shape=pltpu.VMEM((SEQS, ROWS, WIDTH), BF16), i...  38.2 us

profile of v6, /device:TPU:32, one launch (start us, length us, event | category | flops | bytes accessed | tf_op | source)
XLA Modules:
  0.0 38.9 jit_solution(2983098044154332892)
XLA Ops:
  0.0 38.2 %attend.1 = bf16[12,128,128]{2,1,0:T(8,128)(2,1)S(1)} custom-call(bf16[12,128,128]{2,1,0:T(8,128)(2,1)} %bitcast.9, bf16[12,512,128]{2,1,0:T(8,128)(2,1)} %bitcast.7, bf16[12,512,128]{2,1,0:T(8,128)(2,1)} %bitcast.8, bf16[12,32,128]{2,1,0:T(8,128)(2,1)} %bitcast.10, bf16[12,32,128]{2,1,0:T(8,128)(2,1)} %bitcast.11, s32[12,32,32]{2,1,0:T(8,128)} %tm_hbm.1, ...), custom_call_target="tpu_custom_call" | custom-call | tf_op jit(solution)/shard_map/attend/pallas_call | solution.py:430
  38.2 0.7 %copy.9 = bf16[1,12,4,32,128]{4,3,2,1,0:T(8,128)(2,1)} copy(bf16[1,12,4,32,128]{4,3,2,1,0:T(8,128)(2,1)S(1)} %bitcast.6) | data formatting | bytes 786432
